TPU v7x, 256 devices: a whole 4x4x8 slice. The times are simulated.
256 devices in a mesh: replica: 64 (over x, z_hi, y, core), tensor: 4 (over z_lo).
Axes of the slice: x: 4, y: 4, z: 8 (z_hi: 2, z_lo: 4; z = z_hi * 4 + z_lo), core: 2. Of those that a mesh axis runs over, the one named last changes fastest.
Arguments:
- history: bfloat16 [3584, 2, 64, 512], P('replica', None, None, 'tensor')
- new_queries: bfloat16 [3584, 32, 4096], P('replica', 'tensor')
- new_kv: bfloat16 [3584, 32, 4, 2, 128], P('replica', 'tensor'), may hold values from -6 to 6
- norm_gains: bfloat16 [2, 128], replicated, may hold values from 0.5 to 2
- ingest_source: int32 [64], replicated, may hold values from 0 to 63, each once
- new_owner: int32 [3584, 1], replicated, may hold values from 0 to 63, as said below
- history_len: int32 [3584], replicated, may hold values from 1 to 64
- new_len: int32 [3584], replicated, may hold values from 1 to 32
Outputs:
- attended: bfloat16 [3584, 32, 4096], P('replica', 'tensor')
- migrated: bfloat16 [3584, 2, 96, 512], P('replica', None, None, 'tensor')
Inputs may be any that keep to these rules, and one draw needn't show every extreme that they name: Replica j ingests the blocks of the sessions held by replica ingest_source[j], in the same order. `new_owner`: every replica owns exactly 56 sessions after the rebalance. Of the 56 sessions held by one replica (aligned blocks of 56 rows), at most 2 go to any one replica; every replica sends exactly 2 to some replica and receives exactly 2 from some replica, and every replica sends and receives the same counts, in different orders.
All inputs are finite; a program needn't handle non-finite values.
Results may differ from a plain program's by a relative error of at most 0.0078.
Values may be sent and summed in bfloat16 or wider, within the bound.
No kernel may reach another device: no remote copies, remote signals or barrier semaphores. Data moves between devices by JAX's collectives and lax.ppermute only.
A program may use at most 128 MiB of HBM per device.

v0:
```python
import jax
import jax.numpy as jnp
from jax import lax
from jax.sharding import PartitionSpec as P


def rms_scaled(vectors, scaling):
    mean_square = jnp.mean(vectors * vectors, axis=-1, keepdims=True)
    return vectors * lax.rsqrt(mean_square + 1e-06) * scaling


def group_size(slot_count, per_slot):
    group_slots = min(max(1, 2048 // per_slot), slot_count)
    while slot_count % group_slots:
        group_slots -= 1
    return group_slots


def normalize(queries, new_pairs, norm_scale):
    slot_count, block_rows, query_width = queries.shape
    kv_heads = new_pairs.shape[2]
    head_size = new_pairs.shape[4]
    group_heads = query_width // (kv_heads * head_size)
    query_float = queries.reshape(slot_count, block_rows, kv_heads, group_heads, head_size).astype(
        jnp.float32
    )
    query_normed = (
        rms_scaled(query_float, norm_scale[0])
        .astype(jnp.bfloat16)
        .reshape(slot_count, block_rows, query_width)
    )
    key_normed = rms_scaled(new_pairs[:, :, :, 0, :].astype(jnp.float32), norm_scale[1]).astype(
        jnp.bfloat16
    )
    return (query_normed, key_normed, new_pairs[:, :, :, 1, :])


def attend(query_normed, key_normed, new_values, cache, hist_count, new_count):
    slot_count, block_rows, query_width = query_normed.shape
    kv_heads = key_normed.shape[2]
    head_size = key_normed.shape[3]
    group_heads = query_width // (kv_heads * head_size)
    history_rows = cache.shape[2]
    group_slots = group_size(slot_count, block_rows * kv_heads * group_heads)
    group_count = slot_count // group_slots
    score_scale = head_size ** (-0.5)
    positions = jnp.arange(history_rows, dtype=jnp.int32)
    tokens = jnp.arange(block_rows, dtype=jnp.int32)
    causal = tokens[None, :] <= tokens[:, None]

    def one_group(pieces):
        query_block, key_block, value_block, cache_block, hist_block, new_block = pieces
        query_heads = query_block.reshape(group_slots, block_rows, kv_heads, group_heads, head_size)
        hist_keys = cache_block[:, 0].reshape(group_slots, history_rows, kv_heads, head_size)
        hist_values = cache_block[:, 1].reshape(group_slots, history_rows, kv_heads, head_size)
        hist_scores = (
            jnp.einsum(
                "gtkhd,gpkd->gkhtp", query_heads, hist_keys, preferred_element_type=jnp.float32
            )
            * score_scale
        )
        new_scores = (
            jnp.einsum(
                "gtkhd,gukd->gkhtu", query_heads, key_block, preferred_element_type=jnp.float32
            )
            * score_scale
        )
        hist_mask = positions[None, :] < hist_block[:, None]
        hist_scores = jnp.where(hist_mask[:, None, None, None, :], hist_scores, -jnp.inf)
        new_scores = jnp.where(causal[None, None, None], new_scores, -jnp.inf)
        row_max = jnp.maximum(
            jnp.max(hist_scores, axis=-1, keepdims=True),
            jnp.max(new_scores, axis=-1, keepdims=True),
        )
        hist_exp = jnp.exp(hist_scores - row_max)
        new_exp = jnp.exp(new_scores - row_max)
        row_total = jnp.sum(hist_exp, axis=-1, keepdims=True) + jnp.sum(
            new_exp, axis=-1, keepdims=True
        )
        hist_weight = (hist_exp / row_total).astype(jnp.bfloat16)
        new_weight = (new_exp / row_total).astype(jnp.bfloat16)
        mixed_rows = jnp.einsum(
            "gkhtp,gpkd->gtkhd", hist_weight, hist_values, preferred_element_type=jnp.float32
        )
        mixed_rows = mixed_rows + jnp.einsum(
            "gkhtu,gukd->gtkhd", new_weight, value_block, preferred_element_type=jnp.float32
        )
        live_rows = (tokens[None, :] < new_block[:, None]).astype(jnp.float32)
        mixed_rows = mixed_rows * live_rows[:, :, None, None, None]
        return mixed_rows.astype(jnp.bfloat16).reshape(group_slots, block_rows, query_width)

    def grouped(stacked):
        return stacked.reshape((group_count, group_slots) + stacked.shape[1:])

    outputs = lax.map(
        one_group,
        (
            grouped(query_normed),
            grouped(key_normed),
            grouped(new_values),
            grouped(cache),
            grouped(hist_count),
            grouped(new_count),
        ),
    )
    return outputs.reshape(slot_count, block_rows, query_width)


def build_cache(cache, key_normed, new_values, hist_count, new_count):
    slot_count, _, history_rows, kv_width = cache.shape
    block_rows = key_normed.shape[1]
    positions = jnp.arange(history_rows, dtype=jnp.int32)
    tokens = jnp.arange(block_rows, dtype=jnp.int32)
    hist_live = positions[None, :] < hist_count[:, None]
    hist_kept = jnp.where(hist_live[:, None, :, None], cache, jnp.zeros((), jnp.bfloat16))
    fresh_rows = jnp.stack(
        [
            key_normed.reshape(slot_count, block_rows, kv_width),
            new_values.reshape(slot_count, block_rows, kv_width),
        ],
        axis=1,
    )
    new_live = tokens[None, :] < new_count[:, None]
    fresh_rows = jnp.where(new_live[:, None, :, None], fresh_rows, jnp.zeros((), jnp.bfloat16))
    padded = jnp.concatenate(
        [hist_kept, jnp.zeros((slot_count, 2, block_rows, kv_width), jnp.bfloat16)], axis=2
    )

    def place(full_cache, new_piece, start_row):
        zero_index = jnp.zeros((), jnp.int32)
        return lax.dynamic_update_slice(full_cache, new_piece, (zero_index, start_row, zero_index))

    return jax.vmap(place)(padded, fresh_rows, hist_count)


def on_device(
    history, new_queries, new_kv, norm_gains, ingest_source, new_owner, history_len, new_len
):
    replicas = lax.axis_size("replica")
    heads_split = lax.axis_size("tensor")
    own_replica = lax.axis_index("replica")
    sessions = history.shape[0]
    kv_width = history.shape[3]
    head_size = norm_gains.shape[1]
    kv_local = kv_width // head_size
    block_rows = new_queries.shape[1]
    query_all = new_queries.shape[2]
    query_width = query_all // heads_split
    full_rows = block_rows * heads_split
    capacity = max(2, 2 * sessions // replicas)
    norm_scale = norm_gains.astype(jnp.float32)
    replica_ids = jnp.arange(replicas, dtype=jnp.int32)
    counter = jnp.arange(sessions, dtype=jnp.int32)
    owners = new_owner[:, 0].reshape(replicas, sessions)
    earlier = counter[None, :] < counter[:, None]
    same_owner = owners[:, :, None] == owners[:, None, :]
    pair_rank = jnp.sum(jnp.logical_and(same_owner, earlier[None]), axis=2)
    owner_hits = (owners[:, :, None] == replica_ids[None, None, :]).astype(jnp.int32)
    pair_count = jnp.sum(owner_hits, axis=1)
    before = jnp.cumsum(pair_count, axis=0) - pair_count
    owner_slot = jnp.sum(owner_hits * before[:, None, :], axis=2) + pair_rank
    is_mine = owners == own_replica
    slot_picks = jnp.logical_and(
        is_mine[:, :, None], owner_slot[:, :, None] == counter[None, None, :]
    ).astype(jnp.int32)
    slot_holder = jnp.sum(slot_picks * replica_ids[:, None, None], axis=(0, 1))
    slot_rank = jnp.sum(slot_picks * pair_rank[:, :, None], axis=(0, 1))
    global_ids = replica_ids[:, None] * sessions + counter[None, :]
    slot_session = jnp.sum(slot_picks * global_ids[:, :, None], axis=(0, 1))
    ingest_hits = (ingest_source[None, :] == replica_ids[:, None]).astype(jnp.int32)
    ingest_of = jnp.sum(ingest_hits * replica_ids[None, :], axis=1)
    slot_ingest = ingest_of[slot_holder]
    slot_hist = history_len[slot_session]
    slot_new = new_len[slot_session]
    held_owner = owners[own_replica]
    held_rank = pair_rank[own_replica]
    cache_out = (
        jnp.zeros((replicas, capacity) + history.shape[1:], jnp.bfloat16)
        .at[held_owner, held_rank]
        .set(history)
    )
    arrived = lax.all_to_all(cache_out, "replica", split_axis=0, concat_axis=0, tiled=True)
    held_cache = arrived[slot_holder, slot_rank]
    source = ingest_source[own_replica]
    target = owners[source]
    target_rank = pair_rank[source]
    queries_split = new_queries.reshape(sessions, block_rows, heads_split, query_width)
    pairs_split = new_kv.reshape(sessions, block_rows, heads_split, kv_local, 2, head_size)
    query_send = (
        jnp.zeros((replicas, capacity, block_rows, heads_split, query_width), jnp.bfloat16)
        .at[target, target_rank]
        .set(queries_split)
    )
    pair_send = (
        jnp.zeros(
            (replicas, capacity, block_rows, heads_split, kv_local, 2, head_size), jnp.bfloat16
        )
        .at[target, target_rank]
        .set(pairs_split)
    )
    query_in, pair_in = (
        lax.all_to_all(
            lax.all_to_all(query_send, "replica", split_axis=0, concat_axis=0, tiled=True),
            "tensor",
            split_axis=3,
            concat_axis=2,
            tiled=True,
        ),
        lax.all_to_all(
            lax.all_to_all(pair_send, "replica", split_axis=0, concat_axis=0, tiled=True),
            "tensor",
            split_axis=3,
            concat_axis=2,
            tiled=True,
        ),
    )
    query_held = query_in[slot_ingest, slot_rank].reshape(sessions, full_rows, query_width)
    pair_held = pair_in[slot_ingest, slot_rank].reshape(sessions, full_rows, kv_local, 2, head_size)
    query_normed, key_normed, new_values = normalize(query_held, pair_held, norm_scale)
    result = attend(query_normed, key_normed, new_values, held_cache, slot_hist, slot_new)
    migrated = build_cache(held_cache, key_normed, new_values, slot_hist, slot_new)
    result_send = (
        jnp.zeros((replicas, capacity, full_rows, 1, query_width), jnp.bfloat16)
        .at[slot_ingest, slot_rank]
        .set(result.reshape(sessions, full_rows, 1, query_width))
    )
    returned = lax.all_to_all(
        lax.all_to_all(result_send, "replica", split_axis=0, concat_axis=0, tiled=True),
        "tensor",
        split_axis=2,
        concat_axis=3,
        tiled=True,
    )
    attended = returned[target, target_rank].reshape(sessions, block_rows, query_all)
    return (attended, migrated)


def solution(mesh):
    in_specs = (
        P("replica", None, None, "tensor"),
        P("replica", "tensor", None),
        P("replica", "tensor", None, None, None),
        P(),
        P(),
        P(),
        P(),
        P(),
    )
    out_specs = (P("replica", "tensor", None), P("replica", None, None, "tensor"))
    return jax.shard_map(
        on_device, mesh=mesh, in_specs=in_specs, out_specs=out_specs, check_vma=False
    )
```

profile of v0, /device:TPU:1, one launch (start us, length us, event | category | flops | bytes accessed | tf_op | source)
XLA Modules:
  0.0 1436.5 jit_solution(2967319995809411525)
XLA Ops:
  12.6 3.3 scatter_fusion.2
  16.0 55.0 %all_to_all.74 = bf16[64,2,8,4,1,2,128]{6,2,5,3,1,4,0:T(8,128)(2,1)S(1)} all-to-all(bf16[64,2,8,4,1,2,128]{6,2,5,3,1,4,0:T(8,128)(2,1)S(1)} %bitcast.276), channel_id=1, replica_groups=mesh['replica'=64,'tensor'=4] {'replica'}, dimensions={0} | all-to-all | bytes 4194304 | tf_op jit(solution)/shard_map/all_to_all | solution.py:210
  72.7 18.1 %all-to-all-start.4 = ((bf16[64,2,8,4,1,2,128]{6,2,5,1,0,4,3:T(8,128)(2,1)}), bf16[64,2,8,4,1,2,128]{6,2,5,1,0,4,3:T(8,128)(2,1)S(1)}, u32[]{:S(2)}, u32[]{:S(2)}) async-start(bf16[64,2,8,4,1,2,128]{6,2,5,1,0,4,3:T(8,128)(2,1)} %copy.137), calls=%async_computation.4 | async-start | bytes 4194304 | tf_op jit(solution)/shard_map/all_to_all | solution.py:209
  90.8 4.3 broadcast_in_dim.54
  95.1 12.3 scatter_fusion.1
  107.4 31.3 %all-to-all-done.4 = bf16[64,2,8,4,1,2,128]{6,2,5,1,0,4,3:T(8,128)(2,1)S(1)} async-done(((bf16[64,2,8,4,1,2,128]{6,2,5,1,0,4,3:T(8,128)(2,1)}), bf16[64,2,8,4,1,2,128]{6,2,5,1,0,4,3:T(8,128)(2,1)S(1)}, u32[]{:S(2)}, u32[]{:S(2)}) %all-to-all-start.4) | async-done | bytes 2097184 | tf_op jit(solution)/shard_map/all_to_all | solution.py:209
  138.7 6.4 all-to-all-start.1
  148.1 10.5 scatter_fusion
  158.6 177.0 %all-to-all-done.1 = bf16[64,2,8,4,1024]{4,2,3,1,0:T(8,128)(2,1)} async-done(((bf16[64,2,8,4,1024]{4,2,3,1,0:T(8,128)(2,1)}), bf16[64,2,8,4,1024]{4,2,3,1,0:T(8,128)(2,1)}, u32[]{:S(2)}, u32[]{:S(2)}) %all-to-all-start.1) | async-done | bytes 8388640 | tf_op jit(solution)/shard_map/all_to_all | solution.py:203
  335.5 12.0 all-to-all-start
  347.6 8.1 copy.131
  355.6 82.1 %all-to-all-done = bf16[64,2,2,64,128]{4,3,2,1,0:T(8,128)(2,1)} async-done(((bf16[64,2,2,64,128]{4,3,2,1,0:T(8,128)(2,1)}), bf16[64,2,2,64,128]{4,3,2,1,0:T(8,128)(2,1)}, u32[]{:S(2)}, u32[]{:S(2)}) %all-to-all-start) | async-done | bytes 4194336 | tf_op jit(solution)/shard_map/all_to_all | solution.py:182
  437.7 7.7 all-to-all-start.2
  454.1 3.2 gather_fusion.1
  457.4 170.9 %all-to-all-done.2 = bf16[64,2,8,4,1024]{4,2,1,0,3:T(8,128)(2,1)} async-done(((bf16[64,2,8,4,1024]{4,2,1,0,3:T(8,128)(2,1)}), bf16[64,2,8,4,1024]{4,2,1,0,3:T(8,128)(2,1)}, u32[]{:S(2)}, u32[]{:S(2)}) %all-to-all-start.2) | async-done | bytes 8388640 | tf_op jit(solution)/shard_map/all_to_all | solution.py:202
  628.3 8.0 copy.169
  636.3 6.0 gather_fusion.3
  650.5 4.3 mul.207
  654.9 8.9 mul.208
  663.8 7.5 multiply_convert_fusion
  671.4 57.3 %while.13 = (s32[]{:T(128)}, bf16[7,8,32,1024]{3,2,1,0:T(8,128)(2,1)}, bf16[7,8,2,64,128]{4,3,2,1,0:T(8,128)(2,1)S(1)}, s32[7,8]{1,0:T(8,128)S(1)}, bf16[7,8,32,...) while((s32[]{:T(128)}, ...), condition=%wide.region_18.19_spmd.clone, body=%wide.region_13.18_spmd.clone.sunk | while | flops 103020544 | bytes 12904745 | solution.py:95
  728.7 4.3 broadcast.474
  733.0 12.3 scatter_fusion.3
  745.3 9.5 all-to-all-start.5
  757.7 187.5 %all-to-all-done.5 = bf16[64,2,32,1,1024]{4,2,1,3,0:T(8,128)(2,1)} async-done(((bf16[64,2,32,1,1024]{4,2,1,3,0:T(8,128)(2,1)}), bf16[64,2,32,1,1024]{4,2,1,3,0:T(8,128)(2,1)}, u32[]{:S(2)}, u32[]{:S(2)}) %all-to-all-start.5) | async-done | bytes 8388640 | tf_op jit(solution)/shard_map/all_to_all | solution.py:228
  945.2 16.4 %copy.143 = bf16[64,2,32,1,1024]{4,1,0,3,2:T(2,128)(2,1)} copy(bf16[64,2,32,1,1024]{4,2,1,3,0:T(8,128)(2,1)} %all-to-all-done.5) | data formatting | bytes 16777216 | tf_op jit(solution)/shard_map/all_to_all | solution.py:228
  961.6 6.0 all-to-all-start.6
  967.6 446.0 %while.12 = (s32[]{:T(128)}, bf16[56,2,96,128]{3,2,1,0:T(8,128)(2,1)S(1)}, s32[56,4]{0,1:T(4,128)S(1)}, bf16[56,2,32,128]{3,2,0,1:T(8,128)(2,1)}, s32[]{:T(128)}, /*index=5*/s32[4]{0:T(128)S(1)}, s32[]{:T(128)}) while((s32[]{:T(128)}, bf16[56,2,96,128]{3,2,1,0:T(8,128)(2,1)S(1)}, s32[56,4]{0,1:T(4,128)S(1)}, bf16[56,2,32,128]{3,2,0,1:T(8,128)(2,1)}, ...), condition=%wide.while_cond, body=%wide.while_body.sunk | while | flops 8221 | bytes 82115 | solution.py:131
  968.3 3.2 and_reduce_fusion.2
  976.3 3.2 and_reduce_fusion.2
  1008.1 3.2 and_reduce_fusion.2
  1016.1 3.2 and_reduce_fusion.2
  1024.1 3.2 and_reduce_fusion.2
  1048.0 3.2 and_reduce_fusion.2
  1055.9 3.2 and_reduce_fusion.2
  1063.9 3.2 and_reduce_fusion.2
  1087.8 3.2 and_reduce_fusion.2
  1095.7 3.2 and_reduce_fusion.2
  1103.7 3.2 and_reduce_fusion.2
  1111.7 3.2 and_reduce_fusion.2
  1119.6 3.2 and_reduce_fusion.2
  1127.6 3.2 and_reduce_fusion.2
  1135.6 3.2 and_reduce_fusion.2
  1175.4 3.2 and_reduce_fusion.2
  1183.3 3.2 and_reduce_fusion.2
  1191.3 3.2 and_reduce_fusion.2
  1199.3 3.2 and_reduce_fusion.2
  1231.1 3.2 and_reduce_fusion.2
  1239.1 3.2 and_reduce_fusion.2
  1247.0 3.2 and_reduce_fusion.2
  1255.0 3.2 and_reduce_fusion.2
  1263.0 3.2 and_reduce_fusion.2
  1270.9 3.2 and_reduce_fusion.2
  1286.9 3.2 and_reduce_fusion.2
  1294.9 3.2 and_reduce_fusion.2
  1302.8 3.2 and_reduce_fusion.2
  1310.8 3.2 and_reduce_fusion.2
  1358.6 3.2 and_reduce_fusion.2
  1366.5 3.2 and_reduce_fusion.2
  1374.5 3.2 and_reduce_fusion.2
  1382.4 3.2 and_reduce_fusion.2
  1390.4 3.2 and_reduce_fusion.2
  1413.7 16.6 %copy.168 = bf16[64,2,32,1,1024]{4,2,1,0,3:T(8,128)(2,1)} copy(bf16[64,2,32,1,1024]{4,1,0,3,2:T(2,128)(2,1)} %all-to-all-done.6) | data formatting | bytes 16777216 | tf_op jit(solution)/shard_map/all_to_all | solution.py:227
  1430.2 6.1 gather_fusion.6
  (453 shorter events, 426.2 us)
Async XLA Ops:
  0.6 10.7 copy-start
  72.7 66.0 %all-to-all-start.4 = ((bf16[64,2,8,4,1,2,128]{6,2,5,1,0,4,3:T(8,128)(2,1)}), bf16[64,2,8,4,1,2,128]{6,2,5,1,0,4,3:T(8,128)(2,1)S(1)}, u32[]{:S(2)}, u32[]{:S(2)}) async-start(bf16[64,2,8,4,1,2,128]{6,2,5,1,0,4,3:T(8,128)(2,1)} %copy.137), calls=%async_computation.4 | async-start | bytes 4194304 | tf_op jit(solution)/shard_map/all_to_all | solution.py:209
  138.7 196.9 %all-to-all-start.1 = ((bf16[64,2,8,4,1024]{4,2,3,1,0:T(8,128)(2,1)}), bf16[64,2,8,4,1024]{4,2,3,1,0:T(8,128)(2,1)}, u32[]{:S(2)}, u32[]{:S(2)}) async-start(bf16[64,2,8,4,1024]{4,2,3,1,0:T(8,128)(2,1)} %scatter_fusion.1), calls=%async_computation.1 | async-start | bytes 16777216 | tf_op jit(solution)/shard_map/all_to_all | solution.py:203
  335.5 102.2 %all-to-all-start = ((bf16[64,2,2,64,128]{4,3,2,1,0:T(8,128)(2,1)}), bf16[64,2,2,64,128]{4,3,2,1,0:T(8,128)(2,1)}, u32[]{:S(2)}, u32[]{:S(2)}) async-start(bf16[64,2,2,64,128]{4,3,2,1,0:T(8,128)(2,1)} %scatter_fusion), calls=%async_computation | async-start | bytes 8388608 | tf_op jit(solution)/shard_map/all_to_all | solution.py:182
  355.6 89.8 %copy-start.8 = (bf16[2,128]{1,0:T(2,128)(2,1)S(1)}, bf16[2,128]{1,0:T(2,128)(2,1)}, u32[]{:S(2)}) copy-start(bf16[2,128]{1,0:T(2,128)(2,1)} %param.13) | copy-start | bytes 1540
  355.6 89.8 %copy-start.2 = (s32[3584]{0:T(1024)S(1)}, s32[3584]{0:T(1024)}, u32[]{:S(2)}) copy-start(s32[3584]{0:T(1024)} %param.17) | copy-start | bytes 43012
  355.6 90.7 %copy-start.9 = (s32[64]{0:T(128)S(1)}, s32[64]{0:T(128)}, u32[]{:S(2)}) copy-start(s32[64]{0:T(128)} %param.14) | copy-start | bytes 772
  437.7 190.5 %all-to-all-start.2 = ((bf16[64,2,8,4,1024]{4,2,1,0,3:T(8,128)(2,1)}), bf16[64,2,8,4,1024]{4,2,1,0,3:T(8,128)(2,1)}, u32[]{:S(2)}, u32[]{:S(2)}) async-start(bf16[64,2,8,4,1024]{4,2,1,0,3:T(8,128)(2,1)} %copy.131), calls=%async_computation.2 | async-start | bytes 16777216 | tf_op jit(solution)/shard_map/all_to_all | solution.py:202
  451.7 5.7 copy-start.3
  745.3 9.6 copy-start.7
  745.3 9.8 copy-start.4
  745.3 199.9 %all-to-all-start.5 = ((bf16[64,2,32,1,1024]{4,2,1,3,0:T(8,128)(2,1)}), bf16[64,2,32,1,1024]{4,2,1,3,0:T(8,128)(2,1)}, u32[]{:S(2)}, u32[]{:S(2)}) async-start(bf16[64,2,32,1,1024]{4,2,1,3,0:T(8,128)(2,1)} %bitcast.268), calls=%async_computation.5 | async-start | bytes 16777216 | tf_op jit(solution)/shard_map/all_to_all | solution.py:228
  961.6 6.0 copy-start.6
  961.6 452.1 %all-to-all-start.6 = ((bf16[64,2,32,1,1024]{4,1,0,3,2:T(2,128)(2,1)}), bf16[64,2,32,1,1024]{4,1,0,3,2:T(2,128)(2,1)}, u32[]{:S(2)}, u32[]{:S(2)}) async-start(bf16[64,2,32,1,1024]{4,1,0,3,2:T(2,128)(2,1)} %copy.143), calls=%async_computation.6 | async-start | bytes 16777216 | tf_op jit(solution)/shard_map/all_to_all | solution.py:227
  1413.6 16.6 %copy-start.5 = (bf16[56,2,96,128]{3,2,1,0:T(8,128)(2,1)}, bf16[56,2,96,128]{3,2,1,0:T(8,128)(2,1)S(1)}, u32[]{:S(2)}) copy-start(bf16[56,2,96,128]{3,2,1,0:T(8,128)(2,1)S(1)} %get-tuple-element.65) | copy-start | bytes 8257540
  1430.2 6.1 copy-start.1
where the time goes:
time: 1450 us; the launch traced here: 1440 us
  waiting for transfers between devices  649 us (45%)
  other arithmetic  356 us (25%)
  local copies, waits for them, and re-layouts  280 us (19%)
  starting transfers between devices  59.7 us (4%)
  blocking collectives  55 us (4%)
  matrix products  31.3 us (2%)
    scatter x112, other arithmetic  326 us
    all_to_all x1, waiting for transfers between devices, on_device(): lax.all_to_all(result_send, 'replica', split_axis=0, concat_axis=0, tiled...  187 us
    all_to_all x1, waiting for transfers between devices, on_device(): lax.all_to_all(query_send, 'replica', split_axis=0, concat_axis=0, tiled=...  177 us
    all_to_all x1, waiting for transfers between devices, on_device(): lax.all_to_all(lax.all_to_all(query_send, 'replica', split_axis=0, concat...  171 us
    scatter x168, local copies, waits for them, and re-layouts  119 us
    all_to_all x1, waiting for transfers between devices, on_device(): lax.all_to_all(cache_out, 'replica', split_axis=0, concat_axis=0, tiled=T...  82.1 us
    all_to_all x1, blocking collectives, on_device(): lax.all_to_all(pair_send, 'replica', split_axis=0, concat_axis=0, tiled=T...  55 us
    all_to_all x1, waiting for transfers between devices, on_device(): lax.all_to_all(lax.all_to_all(pair_send, 'replica', split_axis=0, concat_...  31.3 us
  transfers between devices with their start and end apart: 6, of which 5 were waited for; matrix products, arithmetic and copies ran while one was open for 35% of the time, Pallas kernels for 0%

commit v1 on v0

v1 whole, which is shorter than its diff:
```python
import functools

import jax
import jax.numpy as jnp
from jax import lax
from jax.experimental import pallas as pl
from jax.experimental.pallas import tpu as pltpu
from jax.sharding import Mesh, PartitionSpec as P

REPLICA = ("x", "zh", "y", "core")
SPREAD = ("zh", "x", "y", "core")
COLUMN = ("x", "y", "core")
RING = ("zh", "zl")
CAP = 2
EPS = 1e-06
BF16 = jnp.bfloat16
F32 = jnp.float32


def spread_index(replica):
    x, zh, y, core = replica // 16, (replica // 8) % 2, (replica // 2) % 4, replica % 2
    return zh * 32 + x * 8 + y * 2 + core


def replica_at(spread):
    zh, x, y, core = spread // 32, (spread // 8) % 4, (spread // 2) % 4, spread % 2
    return x * 16 + zh * 8 + y * 2 + core


def attend_kernel(meta, hist_len, new_len, q_ref, k_ref, v_ref, kv_ref, gain_ref, out_ref):
    halves, blocks = pl.program_id(0), pl.program_id(1)
    count, tokens, width = q_ref.shape
    kv_heads, history, head = k_ref.shape[1], k_ref.shape[4], k_ref.shape[5]
    groups = width // (kv_heads * head)
    rows = groups * tokens
    shards = kv_ref.shape[1]
    fresh = shards * tokens
    keys = history + fresh
    first = (halves * pl.num_programs(1) + blocks) * count
    gain = gain_ref[0:1, :].astype(F32)
    scale = head ** (-0.5)
    column = lax.broadcasted_iota(jnp.int32, (rows, keys), 1)
    token = lax.broadcasted_iota(jnp.int32, (rows, keys), 0) % tokens + meta[1] * tokens
    causal = jnp.logical_and(column >= history, column - history <= token)
    out_token = lax.broadcasted_iota(jnp.int32, (rows, head), 0) % tokens + meta[1] * tokens

    def one_session(s, carry):
        length = hist_len[first + s]
        allowed = jnp.logical_or(causal, column < jnp.minimum(length, history))
        live = out_token < new_len[first + s]
        for h in range(kv_heads):
            lanes = [slice((h * groups + g) * head, (h * groups + g + 1) * head) for g in range(groups)]
            query = jnp.concatenate([q_ref[s, :, lane].astype(F32) for lane in lanes], axis=0)
            mean_square = jnp.mean(query * query, axis=-1, keepdims=True)
            query = (query * lax.rsqrt(mean_square + EPS) * gain).astype(BF16)
            fresh_k = [kv_ref[0, i, h, s, 0].astype(F32) for i in range(shards)]
            fresh_v = [kv_ref[0, i, h, s, 1].astype(F32) for i in range(shards)]
            key = jnp.concatenate([k_ref[0, h, 0, s], jnp.concatenate(fresh_k, axis=0).astype(BF16)], axis=0)
            value = jnp.concatenate([v_ref[0, h, 0, s], jnp.concatenate(fresh_v, axis=0).astype(BF16)], axis=0)
            scores = lax.dot_general(query, key, (((1,), (1,)), ((), ())), preferred_element_type=F32) * scale
            scores = jnp.where(allowed, scores, -jnp.inf)
            peak = jnp.max(scores, axis=-1, keepdims=True)
            weight = jnp.exp(scores - peak)
            weight = (weight / jnp.sum(weight, axis=-1, keepdims=True)).astype(BF16)
            mixed = jnp.dot(weight, value, preferred_element_type=F32)
            mixed = jnp.where(live, mixed, 0.0)
            for g, lane in enumerate(lanes):
                out_ref[s, :, lane] = mixed[g * tokens : (g + 1) * tokens].astype(BF16)
        return carry

    lax.fori_loop(0, count, one_session, 0)


def attend(queries, keys, values, fresh, gains, hist_len, new_len, half, shard):
    sessions, tokens, width = queries.shape
    _, kv_heads, _, per_half, history, head = keys.shape
    shards = fresh.shape[1]
    count = per_half // 4
    blocks = per_half // count
    meta = jnp.stack([half, shard]).astype(jnp.int32)
    whole = lambda i, j, m, a, b: (i * blocks + j, 0, 0)
    cached = pl.BlockSpec((1, kv_heads, 1, count, history, head), lambda i, j, m, a, b: (i, 0, m[0], j, 0, 0))
    return pl.pallas_call(
        attend_kernel,
        out_shape=jax.ShapeDtypeStruct(queries.shape, BF16),
        grid_spec=pltpu.PrefetchScalarGridSpec(
            num_scalar_prefetch=3,
            grid=(2, blocks),
            in_specs=[
                pl.BlockSpec((count, tokens, width), whole),
                cached,
                cached,
                pl.BlockSpec(
                    (1, shards, kv_heads, count, 2, tokens, head),
                    lambda i, j, m, a, b: (m[0], 0, 0, i * blocks + j, 0, 0, 0),
                ),
                pl.BlockSpec((2, head), lambda i, j, m, a, b: (0, 0)),
            ],
            out_specs=pl.BlockSpec((count, tokens, width), whole),
        ),
        compiler_params=pltpu.CompilerParams(vmem_limit_bytes=48 * 1024 * 1024),
    )(meta, hist_len, new_len, queries, keys, values, fresh, gains)


def build_kernel(slot_from, hist_len, new_len, k_ref, v_ref, kv_ref, out_ref):
    count, _, rows, head = out_ref.shape
    history = k_ref.shape[1]
    shards, tokens = kv_ref.shape[1], kv_ref.shape[3]
    target_row = lax.broadcasted_iota(jnp.int32, (rows, rows), 0)
    source = lax.broadcasted_iota(jnp.int32, (rows, rows), 1)

    def one_slot(j, carry):
        at, length, live = slot_from[j], hist_len[j], new_len[j]
        moved = jnp.where(source - history < live, source - history + length, -1)
        target = jnp.where(source < history, jnp.where(source < length, source, -1), moved)
        pick = (target_row == target).astype(F32).astype(BF16)
        fresh = [
            jnp.concatenate([kv_ref[at, i, part].astype(F32) for i in range(shards)], axis=0).astype(BF16)
            for part in range(2)
        ]
        key = jnp.concatenate([k_ref[at], fresh[0]], axis=0)
        value = jnp.concatenate([v_ref[at], fresh[1]], axis=0)
        out_ref[j, 0] = jnp.dot(pick, key, preferred_element_type=F32).astype(BF16)
        out_ref[j, 1] = jnp.dot(pick, value, preferred_element_type=F32).astype(BF16)
        return carry

    lax.fori_loop(0, count, one_slot, 0)


def build(keys, values, fresh, slot_from, hist_len, new_len):
    count = slot_from.shape[0]
    history, head = keys.shape[1:]
    rows = history + fresh.shape[1] * fresh.shape[3]
    vmem = pl.BlockSpec(memory_space=pltpu.VMEM)
    smem = pl.BlockSpec(memory_space=pltpu.SMEM)
    return pl.pallas_call(
        build_kernel,
        out_shape=jax.ShapeDtypeStruct((count, 2, rows, head), BF16),
        in_specs=[smem, smem, smem, vmem, vmem, vmem],
        out_specs=vmem,
        compiler_params=pltpu.CompilerParams(vmem_limit_bytes=48 * 1024 * 1024),
    )(slot_from, hist_len, new_len, keys, values, fresh)


def on_device(history, new_queries, new_kv, norm_gains, ingest_source, new_owner, history_len, new_len):
    sessions, _, hist_rows, head = history.shape
    half_sessions = sessions // 2
    tokens, kv_heads = new_kv.shape[1], new_kv.shape[2]
    half, shard = lax.axis_index("zh"), lax.axis_index("zl")
    me = lax.axis_index(REPLICA)
    column = lax.axis_index(COLUMN)

    raw_key = new_kv[:, :, :, 0, :].astype(F32)
    mean_square = jnp.mean(raw_key * raw_key, axis=-1, keepdims=True)
    normed = (raw_key * lax.rsqrt(mean_square + EPS) * norm_gains[1].astype(F32)).astype(BF16)
    fresh = jnp.stack([normed, new_kv[:, :, :, 1, :]], axis=0).transpose(3, 1, 0, 2, 4)
    fresh_all = lax.all_gather(fresh, RING, axis=0).reshape((2, 4) + fresh.shape)

    source_spread = spread_index(ingest_source[replica_at(jnp.arange(64, dtype=jnp.int32))])
    source_order = source_spread.reshape(2, 32).T.reshape(64)

    def collect(part):
        pieces = part.reshape(64, -1, head)
        spread = lax.all_to_all(pieces, SPREAD, split_axis=0, concat_axis=0, tiled=True)
        picked = jnp.take(spread, source_order, axis=0, mode="clip").reshape(32, 2, -1, head)
        held = lax.all_to_all(picked, COLUMN, split_axis=0, concat_axis=1)
        held = held.reshape(2, half_sessions, hist_rows, head)
        return lax.all_gather(held, RING, axis=0).reshape(2, 4, 2, half_sessions, hist_rows, head)

    keys, values = collect(history[:, 0]), collect(history[:, 1])

    owners = new_owner[:, 0].reshape(64, sessions)
    mine = ingest_source[replica_at(jnp.arange(2, dtype=jnp.int32) * 32 + column)]
    mine_owner = owners[mine]
    order = jnp.arange(sessions, dtype=jnp.int32)
    same = mine_owner[:, :, None] == mine_owner[:, None, :]
    rank = jnp.sum(jnp.logical_and(same, order[None, None, :] < order[None, :, None]), axis=2)
    target = replica_at(half * 32 + jnp.arange(32, dtype=jnp.int32))
    hit = jnp.logical_and(
        mine_owner[None, :, None, :] == target[:, None, None, None],
        rank[None, :, None, :] == jnp.arange(CAP)[None, None, :, None],
    )
    chosen = jnp.sum(jnp.where(hit, order, 0), axis=3).reshape(32, 2 * CAP)
    from_half = (jnp.arange(2 * CAP, dtype=jnp.int32) // CAP)[None, :]
    block = ((chosen // half_sessions) * 4 + shard) * 2 + from_half
    cached_at = (block * half_sessions + chosen % half_sessions).reshape(-1)
    fresh_at = (from_half * 4)[:, :, None] + jnp.arange(4, dtype=jnp.int32)
    fresh_at = ((fresh_at * kv_heads + shard) * sessions + chosen[:, :, None]).reshape(-1)

    def deliver(rows, at):
        sent = jnp.take(rows, at, axis=0, mode="clip").reshape((32, -1) + rows.shape[1:])
        return lax.all_to_all(sent, COLUMN, split_axis=0, concat_axis=0, tiled=True)

    fresh_in = deliver(fresh_all.reshape(-1, 2, tokens, head), fresh_at).reshape(-1, 4, 2, tokens, head)
    keys_in = deliver(keys.reshape(-1, hist_rows, head), cached_at).reshape(-1, hist_rows, head)
    values_in = deliver(values.reshape(-1, hist_rows, head), cached_at).reshape(-1, hist_rows, head)

    all_sessions = jnp.arange(64 * sessions, dtype=jnp.int32)
    owned = new_owner[:, 0] == me
    place = jnp.cumsum(owned.astype(jnp.int32)) - 1
    is_slot = jnp.logical_and(owned[None, :], place[None, :] == order[:, None])

    def of_slot(per_session):
        return jnp.sum(jnp.where(is_slot, per_session[None, :], 0), axis=1)

    slot_session = of_slot(all_sessions)
    slot_hist, slot_new = of_slot(history_len), of_slot(new_len)
    holder = slot_session // sessions
    before = jnp.concatenate([jnp.full((1,), -1, jnp.int32), holder[:-1]])
    slot_rank = (holder == before).astype(jnp.int32)
    replicas = jnp.arange(64, dtype=jnp.int32)
    ingest_at = spread_index(replicas)
    holder_hit = ingest_source[None, :] == holder[:, None]
    ingester = jnp.sum(jnp.where(holder_hit, ingest_at[None, :], 0), axis=1)
    slot_from = (ingester % 32) * (2 * CAP) + (ingester // 32) * CAP + slot_rank

    own_source = ingest_source[me]
    own_hist = lax.dynamic_slice(history_len, (own_source * sessions,), (sessions,))
    own_new = lax.dynamic_slice(new_len, (own_source * sessions,), (sessions,))
    attended = attend(new_queries, keys, values, fresh_all, norm_gains, own_hist, own_new, half, shard)
    migrated = build(keys_in, values_in, fresh_in, slot_from, slot_hist, slot_new)
    return attended, migrated


def solution(mesh):
    split = Mesh(mesh.devices.reshape(4, 2, 4, 2, 4), ("x", "zh", "y", "core", "zl"))
    in_specs = (
        P(REPLICA, None, None, "zl"),
        P(REPLICA, "zl", None),
        P(REPLICA, "zl", None, None, None),
        P(),
        P(),
        P(),
        P(),
        P(),
    )
    out_specs = (P(REPLICA, "zl", None), P(REPLICA, None, None, "zl"))
    return jax.shard_map(on_device, mesh=split, in_specs=in_specs, out_specs=out_specs, check_vma=False)
```

time: 1450 us -> 430 us (0.30)
  waiting for transfers between devices: 649 us -> 157 us
  other arithmetic: 356 us -> 3.99 us
  local copies, waits for them, and re-layouts: 280 us -> 40.5 us
  Pallas kernels: 0 us -> 94.6 us
  matrix products: 31.3 us -> 0 us
  blocking collectives: 55 us -> 83.1 us
  starting transfers between devices: 59.7 us -> 35 us
    all_to_all x6 -> x4, waiting for transfers between devices: 649 us -> 36.8 us  [the longest x1 36.8 us: collect(): lax.all_to_all(pieces, SPREAD, split_axis=0, concat_axis=0, tiled=True)]
    scatter x113 -> x0, other arithmetic: 326 us -> none
    scatter x172 -> x0, local copies, waits for them, and re-layouts: 157 us -> none
    all_gather x0 -> x3, waiting for transfers between devices: none -> 121 us  [the longest x2 121 us: collect(): lax.all_gather(held, RING, axis=0)]
    pallas_call x0 -> x2, Pallas kernels: none -> 94.6 us  [the longest x1 83 us: attend(): pl.pallas_call(attend_kernel, out_shape=jax.ShapeDtypeStruct(queries.shap...]
    all_to_all x6 -> x2, local copies, waits for them, and re-layouts: 52.7 us -> 2.07 us  [collect(): held = lax.all_to_all(picked, COLUMN, split_axis=0, concat_axis=1)]
    dot_general x28 -> x0, matrix products: 31.3 us -> none  [the longest x7 12.5 us: one_group(): jnp.einsum('gtkhd,gukd->gkhtu', query_heads, key_block, preferred_element...]
    all_to_all x1 -> x3, blocking collectives: 55 us -> 83.1 us  [the longest x1 42.4 us: collect(): lax.all_to_all(pieces, SPREAD, split_axis=0, concat_axis=0, tiled=True)]
  transfers between devices with their start and end apart: 6 -> 7, of which waited for: 5 -> 3; matrix products, arithmetic and copies ran while one was open for 35% -> 8% of each run, Pallas kernels for 0% -> 19%
where the time goes in v1:
time: 430 us; the launch traced here: 429 us
  waiting for transfers between devices  157 us (37%)
  Pallas kernels  94.6 us (22%)
  blocking collectives  83.1 us (19%)
  local copies, waits for them, and re-layouts  40.5 us (9%)
  starting transfers between devices  35 us (8%)
  between operations  14.7 us (3%)
    all_gather x2, waiting for transfers between devices, collect(): lax.all_gather(held, RING, axis=0)  121 us
    pallas_call x1, Pallas kernels, attend(): pl.pallas_call(attend_kernel, out_shape=jax.ShapeDtypeStruct(queries.shap...  83 us
    all_to_all x1, blocking collectives, collect(): lax.all_to_all(pieces, SPREAD, split_axis=0, concat_axis=0, tiled=True)  42.4 us
    all_to_all x2, blocking collectives, collect(): held = lax.all_to_all(picked, COLUMN, split_axis=0, concat_axis=1)  40.7 us
    all_to_all x1, waiting for transfers between devices, collect(): lax.all_to_all(pieces, SPREAD, split_axis=0, concat_axis=0, tiled=True)  36.8 us
    all_to_all x3, starting transfers between devices, deliver(): return lax.all_to_all(sent, COLUMN, split_axis=0, concat_axis=0, tiled=True)  19.3 us
    gather x3, local copies, waits for them, and re-layouts, deliver(): jnp.take(rows, at, axis=0, mode='clip').reshape((32, -1) + rows.shape[1:])  15.9 us
    all_to_all x1, starting transfers between devices, collect(): lax.all_to_all(pieces, SPREAD, split_axis=0, concat_axis=0, tiled=True)  15.6 us
  transfers between devices with their start and end apart: 7, of which 3 were waited for; matrix products, arithmetic and copies ran while one was open for 8% of the time, Pallas kernels for 19%

profile of v1, /device:TPU:1, one launch (start us, length us, event | category | flops | bytes accessed | tf_op | source)
XLA Modules:
  0.0 429.5 jit_solution(5224589884512122848)
XLA Ops:
  7.2 3.3 fusion.56
  10.6 0.1 copy.91
  10.7 0.4 fusion.3
  11.1 0.1 copy.77
  11.2 0.1 copy.78
  11.3 0.3 fusion.2
  11.6 1.0 maximum_bitcast_fusion
  12.7 0.5 copy-done.4
  13.1 1.1 fusion.55
  14.2 15.6 %all-to-all-start = ((bf16[64,56,128]{2,1,0:T(8,128)(2,1)}), bf16[64,56,128]{2,1,0:T(8,128)(2,1)S(1)}, u32[]{:S(2)}, u32[]{:S(2)}) async-start(bf16[64,56,128]{2,1,0:T(8,128)(2,1)} %bitcast.3), calls=%async_computation | async-start | bytes 1835008 | tf_op jit(solution)/shard_map/all_to_all | solution.py:164
  30.0 0.8 gather_fusion
  30.7 0.1 gather.32
  30.9 0.1 copy.73
  30.9 0.1 reshape.931
  31.1 36.8 %all-to-all-done = bf16[64,56,128]{2,1,0:T(8,128)(2,1)S(1)} async-done(((bf16[64,56,128]{2,1,0:T(8,128)(2,1)}), bf16[64,56,128]{2,1,0:T(8,128)(2,1)S(1)}, u32[]{:S(2)}, u32[]{:S(2)}) %all-to-all-start) | async-done | bytes 917536 | tf_op jit(solution)/shard_map/all_to_all | solution.py:164
  67.9 0.7 gather_fusion.1
  68.6 20.4 %all_to_all.55 = bf16[32,2,1,56,128]{4,3,1,2,0:T(8,128)(2,1)S(1)} all-to-all(bf16[32,2,1,56,128]{4,3,1,2,0:T(8,128)(2,1)S(1)} %bitcast.77), channel_id=1, replica_groups=mesh['x'=4,'zh'=2,'y'=4,'core'=2,'zl'=4] {'x','y','core'}, dimensions={0} | all-to-all | bytes 1835008 | tf_op jit(solution)/shard_map/all_to_all | solution.py:166
  89.0 1.0 copy.74
  90.0 42.4 %all_to_all.56 = bf16[64,56,128]{2,1,0:T(8,128)(2,1)S(1)} all-to-all(bf16[64,56,128]{2,1,0:T(8,128)(2,1)S(1)} %bitcast.73), channel_id=1, replica_groups=mesh['x'=4,'zh'=2,'y'=4,'core'=2,'zl'=4] {'zh','x','y','core'}, dimensions={0} | all-to-all | bytes 1835008 | tf_op jit(solution)/shard_map/all_to_all | solution.py:164
  132.4 0.7 gather_fusion.2
  133.2 20.4 %all_to_all.57 = bf16[32,2,1,56,128]{4,3,1,2,0:T(8,128)(2,1)S(1)} all-to-all(bf16[32,2,1,56,128]{4,3,1,2,0:T(8,128)(2,1)S(1)} %bitcast.76), channel_id=1, replica_groups=mesh['x'=4,'zh'=2,'y'=4,'core'=2,'zl'=4] {'x','y','core'}, dimensions={0} | all-to-all | bytes 1835008 | tf_op jit(solution)/shard_map/all_to_all | solution.py:166
  153.6 1.1 copy.75
  154.7 0.1 fusion.54
  154.7 0.1 reshape_squeeze.11
  154.9 0.6 gather_fusion.3
  155.5 0.6 gather_fusion.4
  156.1 0.2 convert_reduce_fusion
  156.3 0.1 broadcast_compare_fusion
  156.4 0.2 select_reduce_fusion.3
  156.6 0.1 copy.85
  156.7 0.1 add_multiply_fusion
  156.7 0.1 broadcast_add_fusion
  156.8 0.1 reshape.979
  157.0 8.1 %copy.80 = bf16[32,56,2,8,128]{4,3,2,1,0:T(8,128)(2,1)} copy(bf16[32,56,2,8,128]{4,3,0,1,2:T(8,128)(2,1)} %all-gather.9.cloned.1.call-done) | data formatting | bytes 14680064 | tf_op jit(solution)/shard_map/all_gather | solution.py:157
  165.1 5.5 %gather_fusion.7 = bf16[512,2,8,128]{3,2,1,0:T(8,128)(2,1)} fusion(bf16[1792,2,8,128]{3,2,1,0:T(8,128)(2,1)} %bitcast.63, s32[1024]{0:T(1024)S(1)} %pad_clamp_fusion), kind=kCustom, calls=%fused_computation.7 | custom fusion | bytes 4196352 | tf_op jit(solution)/shard_map/jit(_take)/gather | solution.py:191
  170.6 4.0 all-to-all-start.6
  174.6 0.1 copy.82
  174.7 0.1 rem.547
  174.9 0.1 add.619
  175.0 0.1 copy.83
  175.1 0.2 div.223
  175.3 0.1 copy.81
  175.4 0.2 ne.592
  175.6 50.0 %all-gather.5.cloned.1.call-done = bf16[8,2,28,64,128]{4,3,2,1,0:T(8,128)(2,1)} async-done(((bf16[1,2,28,64,128]{4,3,2,1,0:T(8,128)(2,1)}), bf16[8,2,28,64,128]{4,3,2,1,0:T(8,128)(2,1)}) %all-gather.5.cloned.1.call-update) | async-done | bytes 7340048 | tf_op jit(solution)/shard_map/all_gather | solution.py:168
  225.6 5.2 %gather_fusion.5 = bf16[128,64,128]{2,1,0:T(8,128)(2,1)} fusion(bf16[448,64,128]{2,1,0:T(8,128)(2,1)} %bitcast.65, s32[1024]{0:T(1024)S(1)} %pad_clamp_fusion.1), kind=kCustom, calls=%fused_computation.5 | custom fusion | bytes 4194816 | tf_op jit(solution)/shard_map/jit(_take)/gather | solution.py:191
  230.8 1.4 copy-done.3
  232.2 7.5 %all-to-all-start.4 = ((bf16[32,4,64,128]{3,2,1,0:T(8,128)(2,1)}), bf16[32,4,64,128]{3,2,1,0:T(8,128)(2,1)S(1)}, u32[]{:S(2)}, u32[]{:S(2)}) async-start(bf16[32,4,64,128]{3,2,1,0:T(8,128)(2,1)} %bitcast.72), calls=%async_computation.4 | async-start | bytes 4194304 | tf_op jit(solution)/shard_map/all_to_all | solution.py:192
  239.7 70.6 %all-gather.7.cloned.1.call-done = bf16[8,2,28,64,128]{4,3,2,1,0:T(8,128)(2,1)} async-done(((bf16[1,2,28,64,128]{4,3,2,1,0:T(8,128)(2,1)}), bf16[8,2,28,64,128]{4,3,2,1,0:T(8,128)(2,1)}) %all-gather.7.cloned.1.call-update) | async-done | bytes 7340048 | tf_op jit(solution)/shard_map/all_gather | solution.py:168
  310.3 5.2 %gather_fusion.6 = bf16[128,64,128]{2,1,0:T(8,128)(2,1)} fusion(bf16[448,64,128]{2,1,0:T(8,128)(2,1)} %bitcast.67, s32[1024]{0:T(1024)S(1)} %pad_clamp_fusion.1), kind=kCustom, calls=%fused_computation.6 | custom fusion | bytes 4194816 | tf_op jit(solution)/shard_map/jit(_take)/gather | solution.py:191
  315.5 7.7 %all-to-all-start.5 = ((bf16[32,4,64,128]{3,2,1,0:T(8,128)(2,1)}), bf16[32,4,64,128]{3,2,1,0:T(8,128)(2,1)}, u32[]{:S(2)}, u32[]{:S(2)}) async-start(bf16[32,4,64,128]{3,2,1,0:T(8,128)(2,1)} %bitcast.70), calls=%async_computation.5 | async-start | bytes 4194304 | tf_op jit(solution)/shard_map/all_to_all | solution.py:192
  323.3 0.6 dynamic_slice.9
  324.5 0.1 dynamic_slice.10.hist_len
  324.6 0.1 dynamic_slice.11.new_len
  324.7 0.3 reduce-window.9
  325.0 0.1 slice.49
  325.1 0.1 pad_add_fusion.meta
  325.2 0.1 slice_reduce_fusion
  325.3 0.1 add_bitcast_fusion
  325.4 0.6 select_reduce_fusion
  326.0 0.2 select_reduce_fusion.4
  326.2 0.1 fusion.31.slot_from
  326.3 2.0 copy-done
  328.3 83.0 %shard_map.95 = bf16[56,8,4096]{2,1,0:T(8,128)(2,1)} custom-call(s32[2]{0:T(128)S(1)} %pad_add_fusion.meta, s32[56]{0:T(128)S(1)} %dynamic_slice.10.hist_len, s32[56]{0:T(128)S(1)} %dynamic_slice.11.new_len, bf16[56,8,4096]{2,1,0:T(8,128)(2,1)S(1)} %copy-done, bf16[2,4,2,28,64,128]{5,4,3,2,1,0:T(8,128)(2,1)} %bitcast.66, ...), custom_call_target="tpu_custom_call" | custom-call | tf_op jit(solution)/shard_map/pallas_call | solution.py:83
  411.4 11.6 %shard_map.96 = bf16[56,2,96,128]{3,2,1,0:T(8,128)(2,1)} custom-call(s32[56]{0:T(128)S(1)} %fusion.31.slot_from, s32[56]{0:T(128)S(1)} %get-tuple-element.3.hist_len, s32[56]{0:T(128)S(1)} %get-tuple-element.2.new_len, bf16[128,64,128]{2,1,0:T(8,128)(2,1)S(1)} %bitcast.62, bf16[128,64,128]{2,1,0:T(8,128)(2,1)} %bitcast.32.v_ref, ...), custom_call_target="tpu_custom_call" | custom-call | tf_op jit(solution)/shard_map/pallas_call | solution.py:136
  (48 shorter events, 0.6 us)
Async XLA Ops:
  7.2 3.5 copy-start.1
  7.2 149.8 %all-gather.9.cloned.1.call-start = ((), (), s32[]{:S(2)}) async-start(), calls=%async_computation.9 | async-start | bytes 8257536 | tf_op jit(solution)/shard_map/all_gather | solution.py:157
  11.3 1.8 copy-start.4
  13.1 16.8 %copy-start.2 = (s32[64]{0:T(128)S(1)}, s32[64]{0:T(128)}, u32[]{:S(2)}) copy-start(s32[64]{0:T(128)} %param.12) | copy-start | bytes 772
  14.2 53.6 %all-to-all-start = ((bf16[64,56,128]{2,1,0:T(8,128)(2,1)}), bf16[64,56,128]{2,1,0:T(8,128)(2,1)S(1)}, u32[]{:S(2)}, u32[]{:S(2)}) async-start(bf16[64,56,128]{2,1,0:T(8,128)(2,1)} %bitcast.3), calls=%async_computation | async-start | bytes 1835008 | tf_op jit(solution)/shard_map/all_to_all | solution.py:164
  29.9 195.7 %all-gather.5.cloned.1.call-start = ((), (), s32[]{:S(2)}) async-start(), calls=%async_computation.7 | async-start | bytes 8257536 | tf_op jit(solution)/shard_map/all_gather | solution.py:168
  90.0 220.3 %all-gather.7.cloned.1.call-start = ((), (), s32[]{:S(2)}) async-start(), calls=%async_computation.8 | async-start | bytes 8257536 | tf_op jit(solution)/shard_map/all_gather | solution.py:168
  133.2 21.5 %copy-start.5 = (s32[3584,1]{0,1:T(1,128)S(1)}, s32[3584,1]{0,1:T(1,128)}, u32[]{:S(2)}) copy-start(s32[3584,1]{0,1:T(1,128)} %param.13) | copy-start | bytes 43012
  170.6 60.2 %all-to-all-start.6 = ((bf16[32,16,2,8,128]{4,3,2,1,0:T(8,128)(2,1)}), bf16[32,16,2,8,128]{4,3,2,1,0:T(8,128)(2,1)S(1)}, u32[]{:S(2)}, u32[]{:S(2)}) async-start(bf16[32,16,2,8,128]{4,3,2,1,0:T(8,128)(2,1)} %bitcast.71), calls=%async_computation.6 | async-start | bytes 4194304 | tf_op jit(solution)/shard_map/all_to_all | solution.py:192
  230.8 1.4 copy-start.3
  232.2 83.4 %all-to-all-start.4 = ((bf16[32,4,64,128]{3,2,1,0:T(8,128)(2,1)}), bf16[32,4,64,128]{3,2,1,0:T(8,128)(2,1)S(1)}, u32[]{:S(2)}, u32[]{:S(2)}) async-start(bf16[32,4,64,128]{3,2,1,0:T(8,128)(2,1)} %bitcast.72), calls=%async_computation.4 | async-start | bytes 4194304 | tf_op jit(solution)/shard_map/all_to_all | solution.py:192
  315.5 9.0 %copy-start.6 = (s32[3584]{0:T(1024)S(1)}, s32[3584]{0:T(1024)}, u32[]{:S(2)}) copy-start(s32[3584]{0:T(1024)} %param.14) | copy-start | bytes 43012
  315.5 9.1 %copy-start.7 = (s32[3584]{0:T(1024)S(1)}, s32[3584]{0:T(1024)}, u32[]{:S(2)}) copy-start(s32[3584]{0:T(1024)} %param.15) | copy-start | bytes 43012
  315.5 95.8 %all-to-all-start.5 = ((bf16[32,4,64,128]{3,2,1,0:T(8,128)(2,1)}), bf16[32,4,64,128]{3,2,1,0:T(8,128)(2,1)}, u32[]{:S(2)}, u32[]{:S(2)}) async-start(bf16[32,4,64,128]{3,2,1,0:T(8,128)(2,1)} %bitcast.70), calls=%async_computation.5 | async-start | bytes 4194304 | tf_op jit(solution)/shard_map/all_to_all | solution.py:192
  326.3 2.0 copy-start
Sparse Core Ops, SparseCore 0:
  12.8 127.3 all-gather.8
  142.6 82.9 all-gather.4
  227.4 82.8 all-gather.6

commit v2 on v1

v2 whole, which is shorter than its diff:
```python
import functools

import jax
import jax.numpy as jnp
from jax import lax
from jax.experimental.layout import Layout, with_layout_constraint
from jax.experimental import pallas as pl
from jax.experimental.pallas import tpu as pltpu
from jax.sharding import Mesh, PartitionSpec as P

REPLICA = ("x", "zh", "y", "core")
SPREAD = ("zh", "x", "y", "core")
COLUMN = ("x", "y", "core")
RING = ("zh", "zl")
CAP = 2
EPS = 1e-06
BF16 = jnp.bfloat16
F32 = jnp.float32


def spread_index(replica):
    x, zh, y, core = replica // 16, (replica // 8) % 2, (replica // 2) % 4, replica % 2
    return zh * 32 + x * 8 + y * 2 + core


def replica_at(spread):
    zh, x, y, core = spread // 32, (spread // 8) % 4, (spread // 2) % 4, spread % 2
    return x * 16 + zh * 8 + y * 2 + core


def fresh_rows(ref, index, part):
    shards = ref.shape[1]
    pieces = [ref[(0, i) + index + (part,)].astype(F32) for i in range(shards)]
    return jnp.concatenate(pieces, axis=0).astype(BF16)


def lanes_of(h, groups, head):
    return [slice((h * groups + g) * head, (h * groups + g + 1) * head) for g in range(groups)]


def weigh_kernel(meta, hist_len, q_ref, k_ref, kv_ref, gain_ref, out_ref):
    halves, blocks = pl.program_id(0), pl.program_id(1)
    count, tokens, width = q_ref.shape
    kv_heads, head = k_ref.shape[1], k_ref.shape[5]
    history = k_ref.shape[4]
    groups = width // (kv_heads * head)
    rows = groups * tokens
    fresh = kv_ref.shape[1] * tokens
    keys = out_ref.shape[2]
    first = (halves * pl.num_programs(1) + blocks) * count
    gain = gain_ref[0:1, :].astype(F32)
    scale = head ** (-0.5)
    column = lax.broadcasted_iota(jnp.int32, (kv_heads * rows, keys), 1)
    token = lax.broadcasted_iota(jnp.int32, (kv_heads * rows, keys), 0) % tokens + meta[1] * tokens
    causal = jnp.logical_and(column >= history, column - history <= token)
    padding = jnp.zeros((keys - history - fresh, head), BF16)

    def one_session(s, carry):
        length = jnp.minimum(hist_len[first + s], history)
        allowed = jnp.logical_or(causal, column < length)
        scores = []
        for h in range(kv_heads):
            query = jnp.concatenate([q_ref[s, :, lane].astype(F32) for lane in lanes_of(h, groups, head)], axis=0)
            mean_square = jnp.mean(query * query, axis=-1, keepdims=True)
            query = (query * lax.rsqrt(mean_square + EPS) * gain).astype(BF16)
            key = jnp.concatenate([k_ref[0, h, 0, s], fresh_rows(kv_ref, (h, s), 0), padding], axis=0)
            scores.append(lax.dot_general(query, key, (((1,), (1,)), ((), ())), preferred_element_type=F32))
        scores = jnp.where(allowed, jnp.concatenate(scores, axis=0) * scale, -jnp.inf)
        weight = jnp.exp(scores - jnp.max(scores, axis=-1, keepdims=True))
        out_ref[s] = (weight * (1.0 / jnp.sum(weight, axis=-1, keepdims=True))).astype(BF16)
        return carry

    lax.fori_loop(0, count, one_session, 0, unroll=2)


def mix_kernel(meta, new_len, w_ref, early_ref, late_ref, kv_ref, out_ref):
    halves, blocks = pl.program_id(0), pl.program_id(1)
    count, tokens, width = out_ref.shape
    kv_heads, head = late_ref.shape[1], late_ref.shape[5]
    groups = width // (kv_heads * head)
    rows = groups * tokens
    keys = w_ref.shape[2]
    first = (halves * pl.num_programs(1) + blocks) * count
    used = early_ref.shape[4] + late_ref.shape[4] + kv_ref.shape[1] * tokens
    padding = jnp.zeros((keys - used, head), BF16)
    token = lax.broadcasted_iota(jnp.int32, (rows, head), 0) % tokens + meta[1] * tokens

    def one_session(s, carry):
        live = token < new_len[first + s]
        for h in range(kv_heads):
            pieces = [early_ref[0, h, 0, s], late_ref[0, h, 0, s], fresh_rows(kv_ref, (h, s), 1), padding]
            value = jnp.concatenate(pieces, axis=0)
            mixed = jnp.dot(w_ref[s, h * rows : (h + 1) * rows], value, preferred_element_type=F32)
            mixed = jnp.where(live, mixed, 0.0)
            for g, lane in enumerate(lanes_of(h, groups, head)):
                out_ref[s, :, lane] = mixed[g * tokens : (g + 1) * tokens].astype(BF16)
        return carry

    lax.fori_loop(0, count, one_session, 0, unroll=2)


def cached_spec(part, count, rows, at):
    _, kv_heads, _, _, _, head = part.shape
    return pl.BlockSpec((1, kv_heads, 1, count, rows, head), lambda i, j, m, a: (i, 0, m[0], j, at, 0))


def fresh_spec(fresh, count, blocks):
    _, shards, kv_heads, _, parts, tokens, head = fresh.shape
    return pl.BlockSpec(
        (1, shards, kv_heads, count, parts, tokens, head), lambda i, j, m, a: (m[0], 0, 0, i * blocks + j, 0, 0, 0)
    )


def weigh(queries, early, fresh, gains, hist_len, meta, history):
    sessions, tokens, width = queries.shape
    per_half, _, head = early.shape[3:]
    count = per_half // 2
    blocks = per_half // count
    columns = -(-(history + fresh.shape[1] * tokens) // 128) * 128
    whole = lambda i, j, m, a: (i * blocks + j, 0, 0)
    rows = width // head * tokens
    return pl.pallas_call(
        weigh_kernel,
        out_shape=jax.ShapeDtypeStruct((sessions, rows, columns), BF16),
        grid_spec=pltpu.PrefetchScalarGridSpec(
            num_scalar_prefetch=2,
            grid=(2, blocks),
            in_specs=[
                pl.BlockSpec((count, tokens, width), whole),
                cached_spec(early, count, history, 0),
                fresh_spec(fresh, count, blocks),
                pl.BlockSpec((2, head), lambda i, j, m, a: (0, 0)),
            ],
            out_specs=pl.BlockSpec((count, rows, columns), whole),
        ),
        compiler_params=pltpu.CompilerParams(vmem_limit_bytes=48 * 1024 * 1024),
    )(meta, hist_len, queries, early, fresh, gains)


def mix(weights, early, late, fresh, new_len, meta, width, history):
    sessions = weights.shape[0]
    tokens = fresh.shape[5]
    count = late.shape[3] // 2
    blocks = late.shape[3] // count
    early_rows = early.shape[4] - history
    whole = lambda i, j, m, a: (i * blocks + j, 0, 0)
    return pl.pallas_call(
        mix_kernel,
        out_shape=jax.ShapeDtypeStruct((sessions, tokens, width), BF16),
        grid_spec=pltpu.PrefetchScalarGridSpec(
            num_scalar_prefetch=2,
            grid=(2, blocks),
            in_specs=[
                pl.BlockSpec((count,) + weights.shape[1:], whole),
                cached_spec(early, count, early_rows, history // early_rows),
                cached_spec(late, count, late.shape[4], 0),
                fresh_spec(fresh, count, blocks),
            ],
            out_specs=pl.BlockSpec((count, tokens, width), whole),
        ),
        compiler_params=pltpu.CompilerParams(vmem_limit_bytes=48 * 1024 * 1024),
    )(meta, new_len, weights, early, late, fresh)


def build_kernel(pieces, slot_from, hist_len, new_len, *refs):
    cached_refs, kv_ref, out_ref = refs[:pieces], refs[pieces], refs[-1]
    count, _, rows, head = out_ref.shape
    shards = kv_ref.shape[1]
    tokens = kv_ref.shape[3]
    history = rows - shards * tokens
    target_row = lax.broadcasted_iota(jnp.int32, (rows, rows), 0)
    source = lax.broadcasted_iota(jnp.int32, (rows, rows), 1)

    def one_slot(j, carry):
        at, length, live = slot_from[j], hist_len[j], new_len[j]
        moved = jnp.where(source - history < live, source - history + length, -1)
        target = jnp.where(source < history, jnp.where(source < length, source, -1), moved)
        pick = (target_row == target).astype(F32).astype(BF16)
        fresh = [kv_ref[at, i, 0].astype(F32) for i in range(shards)]
        held = [ref[at] for ref in cached_refs]
        rows_in = jnp.concatenate(held + [jnp.concatenate(fresh, axis=0).astype(BF16)], axis=0)
        out_ref[j, 0] = jnp.dot(pick, rows_in, preferred_element_type=F32).astype(BF16)
        return carry

    lax.fori_loop(0, count, one_slot, 0, unroll=4)


def build(part, pieces, fresh, slot_from, hist_len, new_len, into=None):
    slots, shards, _, tokens, head = fresh.shape
    count = slot_from.shape[0]
    rows = sum(piece[1] for piece in pieces) + shards * tokens
    smem = pl.BlockSpec(memory_space=pltpu.SMEM)
    in_specs = [smem, smem, smem]
    for _, piece_rows, at in pieces:
        in_specs.append(pl.BlockSpec((slots, piece_rows, head), lambda i, at=at: (0, at, 0)))
    in_specs.append(pl.BlockSpec((slots, shards, 1, tokens, head), lambda i: (0, 0, part, 0, 0)))
    operands = [slot_from, hist_len, new_len] + [piece for piece, _, _ in pieces] + [fresh]
    aliases = {}
    if into is not None:
        aliases = {len(in_specs): 0}
        in_specs.append(pl.BlockSpec(memory_space=pl.ANY))
        operands.append(into)
    return pl.pallas_call(
        functools.partial(build_kernel, len(pieces)),
        out_shape=jax.ShapeDtypeStruct((count, 2, rows, head), BF16),
        grid=(1,),
        in_specs=in_specs,
        out_specs=pl.BlockSpec((count, 1, rows, head), lambda i: (0, part, 0, 0)),
        input_output_aliases=aliases,
        compiler_params=pltpu.CompilerParams(vmem_limit_bytes=48 * 1024 * 1024),
    )(*operands)


def on_device(history, new_queries, new_kv, norm_gains, ingest_source, new_owner, history_len, new_len):
    sessions, _, hist_rows, head = history.shape
    half_sessions = sessions // 2
    tokens, kv_heads = new_kv.shape[1], new_kv.shape[2]
    half, shard = lax.axis_index("zh"), lax.axis_index("zl")
    me = lax.axis_index(REPLICA)
    column = lax.axis_index(COLUMN)

    raw_key = new_kv[:, :, :, 0, :].astype(F32)
    mean_square = jnp.mean(raw_key * raw_key, axis=-1, keepdims=True)
    normed = (raw_key * lax.rsqrt(mean_square + EPS) * norm_gains[1].astype(F32)).astype(BF16)
    fresh = jnp.stack([normed, new_kv[:, :, :, 1, :]], axis=0).transpose(3, 1, 0, 2, 4)
    fresh = with_layout_constraint(fresh, Layout(major_to_minor=(0, 1, 2, 3, 4)))

    source_spread = spread_index(ingest_source[replica_at(jnp.arange(64, dtype=jnp.int32))])
    source_order = source_spread.reshape(2, 32).T.reshape(64)

    def spread(part):
        return lax.all_to_all(part.reshape(64, -1, head), SPREAD, split_axis=0, concat_axis=0, tiled=True)

    def gather(pieces):
        picked = jnp.take(pieces, source_order, axis=0, mode="clip").reshape(32, 2, -1, head)
        held = lax.all_to_all(picked, COLUMN, split_axis=0, concat_axis=1)
        return held.reshape(2, half_sessions, -1, head)

    tie = lax.optimization_barrier
    late_rows = hist_rows // 2
    early_rows = hist_rows - late_rows
    both = history.reshape(sessions, 2 * hist_rows, head)
    early_part, late_part, fresh = tie((both[:, :-late_rows], both[:, -late_rows:], fresh))
    early_spread = spread(early_part)
    late_part, early_spread = tie((late_part, early_spread))
    late_spread = spread(late_part)
    early_held = gather(early_spread)
    late_spread, early_held = tie((late_spread, early_held))
    late_held = gather(late_spread)

    fresh_all = lax.all_gather(fresh, RING, axis=0).reshape((2, 4) + fresh.shape)
    early = lax.all_gather(early_held, RING, axis=0).reshape((2, 4) + early_held.shape)
    late = lax.all_gather(late_held, RING, axis=0).reshape((2, 4) + late_held.shape)

    owners = new_owner[:, 0].reshape(64, sessions)
    mine = ingest_source[replica_at(jnp.arange(2, dtype=jnp.int32) * 32 + column)]
    mine_owner = owners[mine]
    order = jnp.arange(sessions, dtype=jnp.int32)
    same = mine_owner[:, :, None] == mine_owner[:, None, :]
    rank = jnp.sum(jnp.logical_and(same, order[None, None, :] < order[None, :, None]), axis=2)
    target = replica_at(half * 32 + jnp.arange(32, dtype=jnp.int32))
    hit = jnp.logical_and(
        mine_owner[None, :, None, :] == target[:, None, None, None],
        rank[None, :, None, :] == jnp.arange(CAP)[None, None, :, None],
    )
    chosen = jnp.sum(jnp.where(hit, order, 0), axis=3).reshape(32, 2 * CAP)
    from_half = (jnp.arange(2 * CAP, dtype=jnp.int32) // CAP)[None, :]
    block = ((chosen // half_sessions) * 4 + shard) * 2 + from_half
    cached_at = (block * half_sessions + chosen % half_sessions).reshape(-1)
    fresh_at = (from_half * 4)[:, :, None] + jnp.arange(4, dtype=jnp.int32)
    fresh_at = ((fresh_at * kv_heads + shard) * sessions + chosen[:, :, None]).reshape(-1)

    def deliver(rows, at):
        sent = jnp.take(rows, at, axis=0, mode="clip").reshape((32, -1) + rows.shape[1:])
        return lax.all_to_all(sent, COLUMN, split_axis=0, concat_axis=0, tiled=True)

    fresh_in = deliver(fresh_all.reshape(-1, 2, tokens, head), fresh_at).reshape(-1, 4, 2, tokens, head)
    def deliver_cached(part):
        rows = part.shape[4]
        return deliver(part.reshape(-1, rows, head), cached_at).reshape(-1, rows, head)

    all_sessions = jnp.arange(64 * sessions, dtype=jnp.int32)
    owned = new_owner[:, 0] == me
    place = jnp.cumsum(owned.astype(jnp.int32)) - 1
    is_slot = jnp.logical_and(owned[None, :], place[None, :] == order[:, None])

    def of_slot(per_session):
        return jnp.sum(jnp.where(is_slot, per_session[None, :], 0), axis=1)

    slot_session = of_slot(all_sessions)
    slot_hist, slot_new = of_slot(history_len), of_slot(new_len)
    holder = slot_session // sessions
    before = jnp.concatenate([jnp.full((1,), -1, jnp.int32), holder[:-1]])
    slot_rank = (holder == before).astype(jnp.int32)
    replicas = jnp.arange(64, dtype=jnp.int32)
    ingest_at = spread_index(replicas)
    holder_hit = ingest_source[None, :] == holder[:, None]
    ingester = jnp.sum(jnp.where(holder_hit, ingest_at[None, :], 0), axis=1)
    slot_from = (ingester % 32) * (2 * CAP) + (ingester // 32) * CAP + slot_rank

    own_source = ingest_source[me]
    own_hist = lax.dynamic_slice(history_len, (own_source * sessions,), (sessions,))
    own_new = lax.dynamic_slice(new_len, (own_source * sessions,), (sessions,))
    meta = jnp.stack([half, shard]).astype(jnp.int32)
    slots = (slot_from, slot_hist, slot_new)
    early, fresh_in = tie((early, fresh_in))
    early_in = deliver_cached(early)
    weights = weigh(new_queries, early, fresh_all, norm_gains, own_hist, meta, hist_rows)
    migrated = build(0, [(early_in, hist_rows, 0)], fresh_in, *slots)
    late, weights = tie((late, weights))
    late_in = deliver_cached(late)
    attended = mix(weights, early, late, fresh_all, own_new, meta, new_queries.shape[2], hist_rows)
    value_pieces = [(early_in, early_rows, hist_rows // early_rows), (late_in, late_rows, 0)]
    migrated = build(1, value_pieces, fresh_in, *slots, into=migrated)
    return attended, migrated


def solution(mesh):
    split = Mesh(mesh.devices.reshape(4, 2, 4, 2, 4), ("x", "zh", "y", "core", "zl"))
    in_specs = (
        P(REPLICA, None, None, "zl"),
        P(REPLICA, "zl", None),
        P(REPLICA, "zl", None, None, None),
        P(),
        P(),
        P(),
        P(),
        P(),
    )
    out_specs = (P(REPLICA, "zl", None), P(REPLICA, None, None, "zl"))
    return jax.shard_map(on_device, mesh=split, in_specs=in_specs, out_specs=out_specs, check_vma=False)
```

time: 430 us -> 357 us (0.83)
  blocking collectives: 83.1 us -> 0 us
  Pallas kernels: 94.6 us -> 34.1 us
  waiting for transfers between devices: 157 us -> 213 us
  starting transfers between devices: 35 us -> 49.9 us
    all_to_all x3 -> x0, blocking collectives: 83.1 us -> none  [the longest x1 42.4 us: collect(): lax.all_to_all(pieces, SPREAD, split_axis=0, concat_axis=0, tiled=True)]
    all_to_all x1 -> x4, waiting for transfers between devices: 36.8 us -> 107 us  [the longest x2 77.9 us: spread(): lax.all_to_all(part.reshape(64, -1, head), SPREAD, split_axis=0, concat_a...]
    pallas_call x2 -> x4, Pallas kernels: 94.6 us -> 34.1 us  [the longest x1 16.2 us: weigh(): pl.pallas_call(weigh_kernel, out_shape=jax.ShapeDtypeStruct((sessions, ro...]
    all_gather x2, waiting for transfers between devices: 121 us -> 77.4 us  [the longest x1 61.5 us: on_device(): lax.all_gather(early_held, RING, axis=0).reshape((2, 4) + early_held.shape)]
    all_to_all x3, waiting for transfers between devices: 0.01 us -> 28.2 us  [deliver(): return lax.all_to_all(sent, COLUMN, split_axis=0, concat_axis=0, tiled=True)]
    all_to_all x1 -> x4, starting transfers between devices: 15.6 us -> 30.8 us  [the longest x2 20.3 us: spread(): lax.all_to_all(part.reshape(64, -1, head), SPREAD, split_axis=0, concat_a...]
    all_gather x1 -> x0, local copies, waits for them, and re-layouts: 8.07 us -> none  [on_device(): lax.all_gather(fresh, RING, axis=0).reshape((2, 4) + fresh.shape)]
    another operation x1 -> x5, local copies, waits for them, and re-layouts: 0.11 us -> 5.53 us  [the longest x2 3.26 us: gather(): held = lax.all_to_all(picked, COLUMN, split_axis=0, concat_axis=1)]
  transfers between devices with their start and end apart: 7 -> 10, of which waited for: 3 -> 9; matrix products, arithmetic and copies ran while one was open for 8% -> 9% of each run, Pallas kernels for 19% -> 8%
where the time goes in v2:
time: 357 us; the launch traced here: 356 us
  waiting for transfers between devices  213 us (60%)
  starting transfers between devices  49.9 us (14%)
  local copies, waits for them, and re-layouts  39.7 us (11%)
  Pallas kernels  34.1 us (10%)
  between operations  14.8 us (4%)
  other arithmetic  4 us (1%)
    all_to_all x2, waiting for transfers between devices, spread(): lax.all_to_all(part.reshape(64, -1, head), SPREAD, split_axis=0, concat_a...  77.9 us
    all_gather x1, waiting for transfers between devices, on_device(): lax.all_gather(early_held, RING, axis=0).reshape((2, 4) + early_held.shape)  61.5 us
    all_to_all x2, waiting for transfers between devices, gather(): held = lax.all_to_all(picked, COLUMN, split_axis=0, concat_axis=1)  29.6 us
    all_to_all x3, waiting for transfers between devices, deliver(): return lax.all_to_all(sent, COLUMN, split_axis=0, concat_axis=0, tiled=True)  28.2 us
    all_to_all x2, starting transfers between devices, spread(): lax.all_to_all(part.reshape(64, -1, head), SPREAD, split_axis=0, concat_a...  20.3 us
    all_to_all x3, starting transfers between devices, deliver(): return lax.all_to_all(sent, COLUMN, split_axis=0, concat_axis=0, tiled=True)  19 us
    pallas_call x1, Pallas kernels, weigh(): pl.pallas_call(weigh_kernel, out_shape=jax.ShapeDtypeStruct((sessions, ro...  16.2 us
    gather x3, local copies, waits for them, and re-layouts, deliver(): jnp.take(rows, at, axis=0, mode='clip').reshape((32, -1) + rows.shape[1:])  16 us
  transfers between devices with their start and end apart: 10, of which 9 were waited for; matrix products, arithmetic and copies ran while one was open for 9% of the time, Pallas kernels for 8%

profile of v2, /device:TPU:1, one launch (start us, length us, event | category | flops | bytes accessed | tf_op | source)
XLA Modules:
  0.0 355.7 jit_solution(18047689804013344842)
XLA Ops:
  7.2 1.5 slice.49
  8.7 1.8 slice.50
  10.6 1.3 fusion.54
  12.0 0.3 fusion.3
  12.4 0.1 copy.66
  12.5 0.3 fusion.2
  12.8 1.1 maximum_bitcast_fusion
  13.9 1.2 reshape.924
  15.2 15.7 %all-to-all-start = ((bf16[64,84,128]{2,1,0:T(8,128)(2,1)}), bf16[64,84,128]{2,1,0:T(8,128)(2,1)S(1)}, u32[]{:S(2)}, u32[]{:S(2)}) async-start(bf16[64,84,128]{2,1,0:T(8,128)(2,1)} %reshape.924), calls=%async_computation | async-start | bytes 2883584 | tf_op jit(solution)/shard_map/all_to_all | solution.py:232
  31.0 0.8 gather_fusion
  31.7 0.1 gather.34
  31.9 0.1 copy.68
  31.9 0.1 reshape.951
  32.1 53.2 %all-to-all-done = bf16[64,84,128]{2,1,0:T(8,128)(2,1)S(1)} async-done(((bf16[64,84,128]{2,1,0:T(8,128)(2,1)}), bf16[64,84,128]{2,1,0:T(8,128)(2,1)S(1)}, u32[]{:S(2)}, u32[]{:S(2)}) %all-to-all-start) | async-done | bytes 1376288 | tf_op jit(solution)/shard_map/all_to_all | solution.py:232
  85.3 0.8 gather_fusion.1
  86.1 2.1 copy.70
  88.3 5.5 %all-to-all-start.2 = ((bf16[32,2,1,84,128]{4,1,3,2,0:T(2,128)(2,1)}), bf16[32,2,1,84,128]{4,1,3,2,0:T(2,128)(2,1)S(1)}, u32[]{:S(2)}, u32[]{:S(2)}) async-start(bf16[32,2,1,84,128]{4,1,3,2,0:T(2,128)(2,1)} %copy.70), calls=%async_computation.2 | async-start | bytes 2752512 | tf_op jit(solution)/shard_map/all_to_all | solution.py:236
  93.8 0.9 reshape.925
  94.7 19.6 %all-to-all-done.2 = bf16[32,2,1,84,128]{4,1,3,2,0:T(2,128)(2,1)S(1)} async-done(((bf16[32,2,1,84,128]{4,1,3,2,0:T(2,128)(2,1)}), bf16[32,2,1,84,128]{4,1,3,2,0:T(2,128)(2,1)S(1)}, u32[]{:S(2)}, u32[]{:S(2)}) %all-to-all-start.2) | async-done | bytes 1376288 | tf_op jit(solution)/shard_map/all_to_all | solution.py:236
  114.3 4.5 %all-to-all-start.1 = ((bf16[64,28,128]{2,1,0:T(8,128)(2,1)}), bf16[64,28,128]{2,1,0:T(8,128)(2,1)S(1)}, u32[]{:S(2)}, u32[]{:S(2)}) async-start(bf16[64,28,128]{2,1,0:T(8,128)(2,1)} %reshape.925), calls=%async_computation.1 | async-start | bytes 1048576 | tf_op jit(solution)/shard_map/all_to_all | solution.py:232
  118.9 1.3 copy.81
  120.1 24.7 %all-to-all-done.1 = bf16[64,28,128]{2,1,0:T(8,128)(2,1)S(1)} async-done(((bf16[64,28,128]{2,1,0:T(8,128)(2,1)}), bf16[64,28,128]{2,1,0:T(8,128)(2,1)S(1)}, u32[]{:S(2)}, u32[]{:S(2)}) %all-to-all-start.1) | async-done | bytes 458784 | tf_op jit(solution)/shard_map/all_to_all | solution.py:232
  144.9 0.6 gather_fusion.3
  145.6 0.7 gather_fusion.2
  146.2 1.1 copy.73
  147.4 5.1 %all-to-all-start.3 = ((bf16[32,2,1,28,128]{4,1,3,2,0:T(2,128)(2,1)}), bf16[32,2,1,28,128]{4,1,3,2,0:T(2,128)(2,1)S(1)}, u32[]{:S(2)}, u32[]{:S(2)}) async-start(bf16[32,2,1,28,128]{4,1,3,2,0:T(2,128)(2,1)} %copy.73), calls=%async_computation.3 | async-start | bytes 917504 | tf_op jit(solution)/shard_map/all_to_all | solution.py:236
  152.7 0.6 gather_fusion.4
  153.3 0.2 convert_reduce_fusion
  153.4 10.0 %all-to-all-done.3 = bf16[32,2,1,28,128]{4,1,3,2,0:T(2,128)(2,1)S(1)} async-done(((bf16[32,2,1,28,128]{4,1,3,2,0:T(2,128)(2,1)}), bf16[32,2,1,28,128]{4,1,3,2,0:T(2,128)(2,1)S(1)}, u32[]{:S(2)}, u32[]{:S(2)}) %all-to-all-start.3) | async-done | bytes 458784 | tf_op jit(solution)/shard_map/all_to_all | solution.py:236
  163.4 0.9 copy.74
  164.4 0.2 select_reduce_fusion.3
  164.6 0.1 copy.75
  164.8 0.1 broadcast_add_fusion
  164.9 0.1 reshape.983
  165.0 5.5 %gather_fusion.5 = bf16[512,2,8,128]{3,2,1,0:T(8,128)(2,1)} fusion(bf16[1792,2,8,128]{3,2,1,0:T(8,128)(2,1)} %bitcast.68, s32[1024]{0:T(1024)S(1)} %pad_clamp_fusion.1), kind=kCustom, calls=%fused_computation.5 | custom fusion | bytes 4196352 | tf_op jit(solution)/shard_map/jit(_take)/gather | solution.py:274
  170.6 3.8 %all-to-all-start.4 = ((bf16[32,16,2,8,128]{4,3,2,1,0:T(8,128)(2,1)}), bf16[32,16,2,8,128]{4,3,2,1,0:T(8,128)(2,1)S(1)}, u32[]{:S(2)}, u32[]{:S(2)}) async-start(bf16[32,16,2,8,128]{4,3,2,1,0:T(8,128)(2,1)} %bitcast.72), calls=%async_computation.4 | async-start | bytes 4194304 | tf_op jit(solution)/shard_map/all_to_all | solution.py:275
  174.4 0.1 copy.77
  174.5 0.1 rem.548
  174.7 0.1 add.629
  174.8 0.1 copy.78
  174.9 0.2 div.224
  175.0 0.1 copy.76
  175.2 0.2 ne.595
  175.3 27.1 %all-to-all-done.4 = bf16[32,16,2,8,128]{4,3,2,1,0:T(8,128)(2,1)S(1)} async-done(((bf16[32,16,2,8,128]{4,3,2,1,0:T(8,128)(2,1)}), bf16[32,16,2,8,128]{4,3,2,1,0:T(8,128)(2,1)S(1)}, u32[]{:S(2)}, u32[]{:S(2)}) %all-to-all-start.4) | async-done | bytes 2097184 | tf_op jit(solution)/shard_map/all_to_all | solution.py:275
  202.5 61.5 %all-gather.8.cloned.1.call-done = bf16[16,28,96,128]{3,2,1,0:T(8,128)(2,1)} async-done(((bf16[2,28,96,128]{3,2,1,0:T(8,128)(2,1)}), bf16[16,28,96,128]{3,2,1,0:T(8,128)(2,1)}) %all-gather.8.cloned.1.call-update) | async-done | bytes 11010064 | tf_op jit(solution)/shard_map/all_gather | solution.py:252
  264.0 6.7 %gather_fusion.6 = bf16[128,96,128]{2,1,0:T(8,128)(2,1)} fusion(bf16[448,96,128]{2,1,0:T(8,128)(2,1)} %bitcast.65, s32[1024]{0:T(1024)S(1)} %pad_clamp_fusion), kind=kCustom, calls=%fused_computation.6 | custom fusion | bytes 6291968 | tf_op jit(solution)/shard_map/jit(_take)/gather | solution.py:274
  270.7 7.7 %all-to-all-start.5 = ((bf16[32,4,96,128]{3,2,1,0:T(8,128)(2,1)}), bf16[32,4,96,128]{3,2,1,0:T(8,128)(2,1)S(1)}, u32[]{:S(2)}, u32[]{:S(2)}) async-start(bf16[32,4,96,128]{3,2,1,0:T(8,128)(2,1)} %bitcast.71), calls=%async_computation.5 | async-start | bytes 6291456 | tf_op jit(solution)/shard_map/all_to_all | solution.py:275
  278.5 0.6 dynamic_slice.9
  279.9 0.3 reduce-window.9
  280.4 0.1 slice_reduce_fusion
  280.5 16.2 %shard_map.95.w_ref = bf16[56,256,128]{2,1,0:T(8,128)(2,1)S(1)} custom-call(s32[2]{0:T(128)S(1)} %pad_add_fusion.meta, s32[56]{0:T(128)S(1)} %dynamic_slice.11.hist_len, bf16[56,8,4096]{2,1,0:T(8,128)(2,1)} %q_ref.1, bf16[2,4,2,28,96,128]{5,4,3,2,1,0:T(8,128)(2,1)} %bitcast.66, bf16[2,4,4,56,2,8,128]{6,5,4,3,2,1,0:T(8,128)(2,1)} %bitcast.69, ...), custom_call_target="tpu_custom_call" | custom-call | tf_op jit(solution)/shard_map/pallas_call | solution.py:122
  296.7 1.8 copy-done.4
  298.6 15.8 %all-gather.6.cloned.1.call-done = bf16[8,2,28,32,128]{4,3,2,1,0:T(8,128)(2,1)} async-done(((bf16[1,2,28,32,128]{4,3,2,1,0:T(8,128)(2,1)}), bf16[8,2,28,32,128]{4,3,2,1,0:T(8,128)(2,1)}) %all-gather.6.cloned.1.call-update) | async-done | bytes 3670032 | tf_op jit(solution)/shard_map/all_gather | solution.py:253
  314.4 3.7 %gather_fusion.7 = bf16[128,32,128]{2,1,0:T(8,128)(2,1)} fusion(bf16[448,32,128]{2,1,0:T(8,128)(2,1)} %bitcast.73, s32[1024]{0:T(1024)S(1)} %pad_clamp_fusion), kind=kCustom, calls=%fused_computation.7 | custom fusion | bytes 2097664 | tf_op jit(solution)/shard_map/jit(_take)/gather | solution.py:274
  318.1 0.1 all-to-all-done.5
  318.2 7.5 %all-to-all-start.6 = ((bf16[32,4,32,128]{3,2,1,0:T(8,128)(2,1)}), bf16[32,4,32,128]{3,2,1,0:T(8,128)(2,1)}, u32[]{:S(2)}, u32[]{:S(2)}) async-start(bf16[32,4,32,128]{3,2,1,0:T(8,128)(2,1)} %bitcast.77), calls=%async_computation.6 | async-start | bytes 2097152 | tf_op jit(solution)/shard_map/all_to_all | solution.py:275
  325.8 0.6 select_reduce_fusion
  326.4 0.2 select_reduce_fusion.4
  326.6 2.0 copy-done.5
  328.7 9.1 %shard_map.96 = bf16[56,8,4096]{2,1,0:T(8,128)(2,1)} custom-call(s32[2]{0:T(128)S(1)} %pad_add_fusion.meta, s32[56]{0:T(128)S(1)} %dynamic_slice.10.new_len, bf16[56,256,128]{2,1,0:T(8,128)(2,1)S(1)} %copy-done.5, bf16[2,4,2,28,96,128]{5,4,3,2,1,0:T(8,128)(2,1)} %bitcast.67, bf16[2,4,2,28,32,128]{5,4,3,2,1,0:T(8,128)(2,1)} %bitcast.74, ...), custom_call_target="tpu_custom_call" | custom-call | tf_op jit(solution)/shard_map/pallas_call | solution.py:147
  337.7 3.9 %shard_map.97.refs_3_ = bf16[56,2,96,128]{3,2,1,0:T(8,128)(2,1)} custom-call(s32[56]{0:T(128)S(1)} %fusion.39.slot_from, s32[56]{0:T(128)S(1)} %get-tuple-element.25.hist_len, s32[56]{0:T(128)S(1)} %get-tuple-element.24.new_len, bf16[128,96,128]{2,1,0:T(8,128)(2,1)S(1)} %bitcast.61, bf16[128,4,2,8,128]{4,3,2,1,0:T(8,128)(2,1)S(1)} %bitcast.63), custom_call_target="tpu_custom_call" | custom-call | tf_op jit(solution)/shard_map/pallas_call | solution.py:203
  341.7 1.0 all-to-all-done.6
  342.6 1.6 copy-done.3
  344.2 4.9 %shard_map.98 = bf16[56,2,96,128]{3,2,1,0:T(8,128)(2,1)} custom-call(s32[56]{0:T(128)S(1)} %fusion.39.slot_from, s32[56]{0:T(128)S(1)} %get-tuple-element.25.hist_len, s32[56]{0:T(128)S(1)} %get-tuple-element.24.new_len, bf16[128,96,128]{2,1,0:T(8,128)(2,1)} %bitcast.62, bf16[128,32,128]{2,1,0:T(8,128)(2,1)} %bitcast.35.refs_1_, ...), custom_call_target="tpu_custom_call", output_to_operand_aliasing={{}: (6, {})} | custom-call | tf_op jit(solution)/shard_map/pallas_call | solution.py:203
  (67 shorter events, 1.5 us)
Async XLA Ops:
  7.2 3.4 copy-start.8
  7.2 157.8 %all-gather.10.cloned.1.call-start = ((), (), s32[]{:S(2)}) async-start(), calls=%async_computation.9 | async-start | bytes 8257536 | tf_op jit(solution)/shard_map/all_gather | solution.py:251
  10.6 1.4 copy-start.6
  15.2 15.8 %copy-start.7 = (s32[64]{0:T(128)S(1)}, s32[64]{0:T(128)}, u32[]{:S(2)}) copy-start(s32[64]{0:T(128)} %param.12) | copy-start | bytes 772
  15.2 70.1 %all-to-all-start = ((bf16[64,84,128]{2,1,0:T(8,128)(2,1)}), bf16[64,84,128]{2,1,0:T(8,128)(2,1)S(1)}, u32[]{:S(2)}, u32[]{:S(2)}) async-start(bf16[64,84,128]{2,1,0:T(8,128)(2,1)} %reshape.924), calls=%async_computation | async-start | bytes 2883584 | tf_op jit(solution)/shard_map/all_to_all | solution.py:232
  86.1 7.7 %copy-start.9 = (bf16[56,32,128]{2,1,0:T(8,128)(2,1)S(1)}, bf16[56,32,128]{2,1,0:T(8,128)(2,1)}, u32[]{:S(2)}) copy-start(bf16[56,32,128]{2,1,0:T(8,128)(2,1)} %slice.50) | copy-start | bytes 1376260
  88.3 26.0 %all-to-all-start.2 = ((bf16[32,2,1,84,128]{4,1,3,2,0:T(2,128)(2,1)}), bf16[32,2,1,84,128]{4,1,3,2,0:T(2,128)(2,1)S(1)}, u32[]{:S(2)}, u32[]{:S(2)}) async-start(bf16[32,2,1,84,128]{4,1,3,2,0:T(2,128)(2,1)} %copy.70), calls=%async_computation.2 | async-start | bytes 2752512 | tf_op jit(solution)/shard_map/all_to_all | solution.py:236
  114.3 30.6 %all-to-all-start.1 = ((bf16[64,28,128]{2,1,0:T(8,128)(2,1)}), bf16[64,28,128]{2,1,0:T(8,128)(2,1)S(1)}, u32[]{:S(2)}, u32[]{:S(2)}) async-start(bf16[64,28,128]{2,1,0:T(8,128)(2,1)} %reshape.925), calls=%async_computation.1 | async-start | bytes 1048576 | tf_op jit(solution)/shard_map/all_to_all | solution.py:232
  118.8 145.2 %all-gather.8.cloned.1.call-start = ((), (), s32[]{:S(2)}) async-start(), calls=%async_computation.8 | async-start | bytes 12386304 | tf_op jit(solution)/shard_map/all_gather | solution.py:252
  144.9 7.6 %copy-start.10 = (s32[3584,1]{0,1:T(1,128)S(1)}, s32[3584,1]{0,1:T(1,128)}, u32[]{:S(2)}) copy-start(s32[3584,1]{0,1:T(1,128)} %param.13) | copy-start | bytes 43012
  147.4 16.0 %all-to-all-start.3 = ((bf16[32,2,1,28,128]{4,1,3,2,0:T(2,128)(2,1)}), bf16[32,2,1,28,128]{4,1,3,2,0:T(2,128)(2,1)S(1)}, u32[]{:S(2)}, u32[]{:S(2)}) async-start(bf16[32,2,1,28,128]{4,1,3,2,0:T(2,128)(2,1)} %copy.73), calls=%async_computation.3 | async-start | bytes 917504 | tf_op jit(solution)/shard_map/all_to_all | solution.py:236
  152.4 161.9 %all-gather.6.cloned.1.call-start = ((), (), s32[]{:S(2)}) async-start(), calls=%async_computation.7 | async-start | bytes 4128768 | tf_op jit(solution)/shard_map/all_gather | solution.py:253
  170.6 31.9 %all-to-all-start.4 = ((bf16[32,16,2,8,128]{4,3,2,1,0:T(8,128)(2,1)}), bf16[32,16,2,8,128]{4,3,2,1,0:T(8,128)(2,1)S(1)}, u32[]{:S(2)}, u32[]{:S(2)}) async-start(bf16[32,16,2,8,128]{4,3,2,1,0:T(8,128)(2,1)} %bitcast.72), calls=%async_computation.4 | async-start | bytes 4194304 | tf_op jit(solution)/shard_map/all_to_all | solution.py:275
  202.5 68.3 %copy-start.1 = (bf16[32,16,2,8,128]{4,3,2,1,0:T(8,128)(2,1)}, bf16[32,16,2,8,128]{4,3,2,1,0:T(8,128)(2,1)S(1)}, u32[]{:S(2)}) copy-start(bf16[32,16,2,8,128]{4,3,2,1,0:T(8,128)(2,1)S(1)} %all-to-all-done.4) | copy-start | bytes 6291460
  270.7 9.0 %copy-start.11 = (s32[3584]{0:T(1024)S(1)}, s32[3584]{0:T(1024)}, u32[]{:S(2)}) copy-start(s32[3584]{0:T(1024)} %param.15) | copy-start | bytes 43012
  270.7 9.1 %copy-start.12 = (s32[3584]{0:T(1024)S(1)}, s32[3584]{0:T(1024)}, u32[]{:S(2)}) copy-start(s32[3584]{0:T(1024)} %param.14) | copy-start | bytes 43012
  270.7 47.5 %all-to-all-start.5 = ((bf16[32,4,96,128]{3,2,1,0:T(8,128)(2,1)}), bf16[32,4,96,128]{3,2,1,0:T(8,128)(2,1)S(1)}, u32[]{:S(2)}, u32[]{:S(2)}) async-start(bf16[32,4,96,128]{3,2,1,0:T(8,128)(2,1)} %bitcast.71), calls=%async_computation.5 | async-start | bytes 6291456 | tf_op jit(solution)/shard_map/all_to_all | solution.py:275
  296.7 1.8 copy-start.4
  318.2 19.5 %copy-start = (bf16[32,4,96,128]{3,2,1,0:T(8,128)(2,1)}, bf16[32,4,96,128]{3,2,1,0:T(8,128)(2,1)S(1)}, u32[]{:S(2)}) copy-start(bf16[32,4,96,128]{3,2,1,0:T(8,128)(2,1)S(1)} %all-to-all-done.5) | copy-start | bytes 9437188
  318.2 24.4 %all-to-all-start.6 = ((bf16[32,4,32,128]{3,2,1,0:T(8,128)(2,1)}), bf16[32,4,32,128]{3,2,1,0:T(8,128)(2,1)}, u32[]{:S(2)}, u32[]{:S(2)}) async-start(bf16[32,4,32,128]{3,2,1,0:T(8,128)(2,1)} %bitcast.77), calls=%async_computation.6 | async-start | bytes 2097152 | tf_op jit(solution)/shard_map/all_to_all | solution.py:275
  326.6 2.0 copy-start.5
  328.7 9.1 %copy-start.2 = (bf16[32,16,2,8,128]{4,3,2,1,0:T(8,128)(2,1)S(1)}, bf16[32,16,2,8,128]{4,3,2,1,0:T(8,128)(2,1)}, u32[]{:S(2)}) copy-start(bf16[32,16,2,8,128]{4,3,2,1,0:T(8,128)(2,1)} %copy-done.1) | copy-start | bytes 6291460
  342.6 1.6 copy-start.3
Sparse Core Ops, SparseCore 0:
  14.1 130.2 all-gather.9
  146.7 117.2 all-gather.7
  265.8 48.5 all-gather.5

commit v3 on v2

v3 whole, which is shorter than its diff:
```python
import functools

import jax
import jax.numpy as jnp
from jax import lax
from jax.experimental.layout import Layout, with_layout_constraint
from jax.experimental import pallas as pl
from jax.experimental.pallas import tpu as pltpu
from jax.sharding import Mesh, PartitionSpec as P

REPLICA = ("x", "zh", "y", "core")
SPREAD = ("zh", "x", "y", "core")
COLUMN = ("x", "y", "core")
RING = ("zh", "zl")
CAP = 2
SHARDS = 4
UNIT = 16
UNITS = 4
KEPT = 24
EPS = 1e-06
BF16 = jnp.bfloat16
F32 = jnp.float32


def spread_index(replica):
    x, zh, y, core = replica // 16, (replica // 8) % 2, (replica // 2) % 4, replica % 2
    return zh * 32 + x * 8 + y * 2 + core


def replica_at(spread):
    zh, x, y, core = spread // 32, (spread // 8) % 4, (spread // 2) % 4, spread % 2
    return x * 16 + zh * 8 + y * 2 + core


def fresh_rows(ref, index, part):
    shards = ref.shape[1]
    pieces = [ref[(0, i) + index + (part,)].astype(F32) for i in range(shards)]
    return jnp.concatenate(pieces, axis=0).astype(BF16)


def lanes_of(h, groups, head):
    return [slice((h * groups + g) * head, (h * groups + g + 1) * head) for g in range(groups)]


def unit_place(ref, first, step):
    per_half = ref.shape[3]
    at = jnp.minimum(first + step, 2 * per_half - 1)
    upper = (at >= per_half).astype(jnp.int32)
    return upper, at - upper * per_half


def weigh_kernel(meta, hist_len, unit_first, q_ref, early_ref, kv_ref, gain_ref, out_ref):
    count, tokens, width = q_ref.shape
    kv_heads, head = early_ref.shape[1], early_ref.shape[5]
    groups = width // (kv_heads * head)
    rows = groups * tokens
    fresh = kv_ref.shape[1] * tokens
    keys = out_ref.shape[2]
    history = UNITS * UNIT
    first = pl.program_id(0) * count
    gain = gain_ref[0:1, :].astype(F32)
    scale = head ** (-0.5)
    column = lax.broadcasted_iota(jnp.int32, (kv_heads * rows, keys), 1)
    token = lax.broadcasted_iota(jnp.int32, (kv_heads * rows, keys), 0) % tokens + meta[1] * tokens
    causal = jnp.logical_and(column >= history, column - history <= token)
    padding = jnp.zeros((keys - history - fresh, head), BF16)

    def one_session(s, carry):
        length = jnp.minimum(hist_len[first + s], history)
        allowed = jnp.logical_or(causal, column < length)
        places = [unit_place(early_ref, unit_first[first + s], q) for q in range(UNITS)]
        scores = []
        for h in range(kv_heads):
            query = jnp.concatenate([q_ref[s, :, lane].astype(F32) for lane in lanes_of(h, groups, head)], axis=0)
            mean_square = jnp.mean(query * query, axis=-1, keepdims=True)
            query = (query * lax.rsqrt(mean_square + EPS) * gain).astype(BF16)
            cached = [early_ref[upper, h, 0, at, 0:UNIT, :] for upper, at in places]
            key = jnp.concatenate(cached + [fresh_rows(kv_ref, (h, s), 0), padding], axis=0)
            scores.append(lax.dot_general(query, key, (((1,), (1,)), ((), ())), preferred_element_type=F32))
        scores = jnp.where(allowed, jnp.concatenate(scores, axis=0) * scale, -jnp.inf)
        weight = jnp.exp(scores - jnp.max(scores, axis=-1, keepdims=True))
        out_ref[s] = (weight * (1.0 / jnp.sum(weight, axis=-1, keepdims=True))).astype(BF16)
        return carry

    lax.fori_loop(0, count, one_session, 0, unroll=2)


def mix_kernel(meta, new_len, unit_first, w_ref, early_ref, late_ref, kv_ref, out_ref):
    count, tokens, width = out_ref.shape
    kv_heads, head = late_ref.shape[1], late_ref.shape[5]
    groups = width // (kv_heads * head)
    rows = groups * tokens
    keys = w_ref.shape[2]
    first = pl.program_id(0) * count
    fresh = kv_ref.shape[1] * tokens
    padding = jnp.zeros((keys - UNITS * UNIT - fresh, head), BF16)
    token = lax.broadcasted_iota(jnp.int32, (rows, head), 0) % tokens + meta[1] * tokens

    def one_session(s, carry):
        live = token < new_len[first + s]
        places = [unit_place(late_ref, unit_first[first + s], q) for q in range(UNITS)]
        for h in range(kv_heads):
            cached = []
            for upper, at in places:
                cached.append(early_ref[upper, h, 0, at, UNIT:KEPT, :].astype(F32))
                cached.append(late_ref[upper, h, 0, at].astype(F32))
            cached = jnp.concatenate(cached, axis=0).astype(BF16)
            value = jnp.concatenate([cached, fresh_rows(kv_ref, (h, s), 1), padding], axis=0)
            mixed = jnp.dot(w_ref[s, h * rows : (h + 1) * rows], value, preferred_element_type=F32)
            mixed = jnp.where(live, mixed, 0.0)
            for g, lane in enumerate(lanes_of(h, groups, head)):
                out_ref[s, :, lane] = mixed[g * tokens : (g + 1) * tokens].astype(BF16)
        return carry

    lax.fori_loop(0, count, one_session, 0, unroll=2)


def units_spec(part):
    halves, kv_heads, _, per_half, rows, head = part.shape
    return pl.BlockSpec((halves, kv_heads, 1, per_half, rows, head), lambda i, m, a, b: (0, 0, m[0], 0, 0, 0))


def fresh_spec(fresh, count):
    _, shards, kv_heads, _, parts, tokens, head = fresh.shape
    return pl.BlockSpec((1, shards, kv_heads, count, parts, tokens, head), lambda i, m, a, b: (m[0], 0, 0, i, 0, 0, 0))


def weigh(queries, early, fresh, gains, hist_len, unit_first, meta):
    sessions, tokens, width = queries.shape
    head = early.shape[5]
    count = sessions // 4
    columns = -(-(UNITS * UNIT + fresh.shape[1] * tokens) // 128) * 128
    whole = lambda i, m, a, b: (i, 0, 0)
    rows = width // head * tokens
    return pl.pallas_call(
        weigh_kernel,
        out_shape=jax.ShapeDtypeStruct((sessions, rows, columns), BF16),
        grid_spec=pltpu.PrefetchScalarGridSpec(
            num_scalar_prefetch=3,
            grid=(sessions // count,),
            in_specs=[
                pl.BlockSpec((count, tokens, width), whole),
                units_spec(early),
                fresh_spec(fresh, count),
                pl.BlockSpec((2, head), lambda i, m, a, b: (0, 0)),
            ],
            out_specs=pl.BlockSpec((count, rows, columns), whole),
        ),
        compiler_params=pltpu.CompilerParams(vmem_limit_bytes=48 * 1024 * 1024),
    )(meta, hist_len, unit_first, queries, early, fresh, gains)


def mix(weights, early, late, fresh, new_len, unit_first, meta, width):
    sessions = weights.shape[0]
    tokens = fresh.shape[5]
    count = sessions // 4
    whole = lambda i, m, a, b: (i, 0, 0)
    return pl.pallas_call(
        mix_kernel,
        out_shape=jax.ShapeDtypeStruct((sessions, tokens, width), BF16),
        grid_spec=pltpu.PrefetchScalarGridSpec(
            num_scalar_prefetch=3,
            grid=(sessions // count,),
            in_specs=[
                pl.BlockSpec((count,) + weights.shape[1:], whole),
                units_spec(early),
                units_spec(late),
                fresh_spec(fresh, count),
            ],
            out_specs=pl.BlockSpec((count, tokens, width), whole),
        ),
        compiler_params=pltpu.CompilerParams(vmem_limit_bytes=48 * 1024 * 1024),
    )(meta, new_len, unit_first, weights, early, late, fresh)


def build_kernel(part, slot_from, hist_len, new_len, *refs):
    cached_refs, kv_ref, out_ref = refs[: part + 1], refs[part + 1], refs[-1]
    count, _, rows, head = out_ref.shape
    shards = kv_ref.shape[1]
    tokens = kv_ref.shape[3]
    history = rows - shards * tokens
    target_row = lax.broadcasted_iota(jnp.int32, (rows, rows), 0)
    source = lax.broadcasted_iota(jnp.int32, (rows, rows), 1)

    def one_slot(j, carry):
        at, length, live = slot_from[j], hist_len[j], new_len[j]
        moved = jnp.where(source - history < live, source - history + length, -1)
        target = jnp.where(source < history, jnp.where(source < length, source, -1), moved)
        pick = (target_row == target).astype(F32).astype(BF16)
        rows_in = []
        for q in range(UNITS):
            if part == 0:
                rows_in.append(cached_refs[0][at, q, 0:UNIT, :].astype(F32))
            else:
                rows_in.append(cached_refs[0][at, q, UNIT:KEPT, :].astype(F32))
                rows_in.append(cached_refs[1][at, q].astype(F32))
        rows_in += [kv_ref[at, i, 0].astype(F32) for i in range(shards)]
        rows_in = jnp.concatenate(rows_in, axis=0).astype(BF16)
        out_ref[j, 0] = jnp.dot(pick, rows_in, preferred_element_type=F32).astype(BF16)
        return carry

    lax.fori_loop(0, count, one_slot, 0, unroll=4)


def build(part, pieces, fresh, slot_from, hist_len, new_len, into=None):
    slots, shards, _, tokens, head = fresh.shape
    count = slot_from.shape[0]
    rows = UNITS * UNIT + shards * tokens
    smem = pl.BlockSpec(memory_space=pltpu.SMEM)
    in_specs = [smem, smem, smem]
    for piece in pieces:
        in_specs.append(pl.BlockSpec(piece.shape, lambda i: (0, 0, 0, 0)))
    in_specs.append(pl.BlockSpec((slots, shards, 1, tokens, head), lambda i: (0, 0, part, 0, 0)))
    operands = [slot_from, hist_len, new_len, *pieces, fresh]
    aliases = {}
    if into is not None:
        aliases = {len(in_specs): 0}
        in_specs.append(pl.BlockSpec(memory_space=pl.ANY))
        operands.append(into)
    return pl.pallas_call(
        functools.partial(build_kernel, part),
        out_shape=jax.ShapeDtypeStruct((count, 2, rows, head), BF16),
        grid=(1,),
        in_specs=in_specs,
        out_specs=pl.BlockSpec((count, 1, rows, head), lambda i: (0, part, 0, 0)),
        input_output_aliases=aliases,
        compiler_params=pltpu.CompilerParams(vmem_limit_bytes=48 * 1024 * 1024),
    )(*operands)


def units_of(lengths):
    return (lengths + UNIT - 1) // UNIT


def run(capacity, history, new_queries, new_kv, norm_gains, ingest_source, new_owner, history_len, new_len):
    sessions, _, hist_rows, head = history.shape
    per_half = capacity // 2
    tokens, kv_heads = new_kv.shape[1], new_kv.shape[2]
    half, shard = lax.axis_index("zh"), lax.axis_index("zl")
    me = lax.axis_index(REPLICA)
    column = lax.axis_index(COLUMN)
    tie = lax.optimization_barrier
    lengths = history_len.reshape(64, sessions)

    raw_key = new_kv[:, :, :, 0, :].astype(F32)
    mean_square = jnp.mean(raw_key * raw_key, axis=-1, keepdims=True)
    normed = (raw_key * lax.rsqrt(mean_square + EPS) * norm_gains[1].astype(F32)).astype(BF16)
    fresh = jnp.stack([normed, new_kv[:, :, :, 1, :]], axis=0).transpose(3, 1, 0, 2, 4)
    fresh = with_layout_constraint(fresh, Layout(major_to_minor=(0, 1, 2, 3, 4)))

    held_units = units_of(lax.dynamic_slice(history_len, (me * sessions,), (sessions,)))
    slot = jnp.arange(capacity, dtype=jnp.int32)
    passed = jnp.cumsum(held_units)[None, :] <= slot[:, None]
    unit_session = jnp.minimum(jnp.sum(passed.astype(jnp.int32), axis=1), sessions - 1)
    unit_step = jnp.clip(slot - jnp.sum(jnp.where(passed, held_units[None, :], 0), axis=1), 0, UNITS - 1)
    key_unit = unit_session * (2 * UNITS) + unit_step
    fresh, key_unit = tie((fresh, key_unit))
    fresh_all = lax.all_gather(fresh, RING, axis=0).reshape((2, SHARDS) + fresh.shape)
    cached = history.reshape(-1, UNIT, head)
    packed_keys = jnp.take(cached, key_unit, axis=0, mode="clip")
    packed_values = jnp.take(cached, key_unit + UNITS, axis=0, mode="clip")

    source_spread = spread_index(ingest_source[replica_at(jnp.arange(64, dtype=jnp.int32))])
    source_order = source_spread.reshape(2, 32).T.reshape(64)

    def spread(part):
        return lax.all_to_all(part.reshape(64, -1, head), SPREAD, split_axis=0, concat_axis=0, tiled=True)

    def gather(pieces, rows):
        picked = jnp.take(pieces, source_order, axis=0, mode="clip").reshape(32, 2, -1, head)
        held = lax.all_to_all(picked, COLUMN, split_axis=0, concat_axis=1)
        return held.reshape(2, per_half, rows, head)

    early_part = jnp.concatenate([packed_keys, packed_values[:, : KEPT - UNIT]], axis=1)
    late_part = packed_values[:, KEPT - UNIT :]
    early_spread = spread(early_part)
    late_part, early_spread = tie((late_part, early_spread))
    late_spread = spread(late_part)
    early_held = gather(early_spread, KEPT)
    late_spread, early_held = tie((late_spread, early_held))
    late_held = gather(late_spread, 2 * UNIT - KEPT)
    early = lax.all_gather(early_held, RING, axis=0).reshape((2, SHARDS) + early_held.shape)
    late = lax.all_gather(late_held, RING, axis=0).reshape((2, SHARDS) + late_held.shape)

    owners = new_owner[:, 0].reshape(64, sessions)
    mine = ingest_source[replica_at(jnp.arange(2, dtype=jnp.int32) * 32 + column)]
    mine_owner = owners[mine]
    order = jnp.arange(sessions, dtype=jnp.int32)
    same = mine_owner[:, :, None] == mine_owner[:, None, :]
    rank = jnp.sum(jnp.logical_and(same, order[None, None, :] < order[None, :, None]), axis=2)
    target = replica_at(half * 32 + jnp.arange(32, dtype=jnp.int32))
    hit = jnp.logical_and(
        mine_owner[None, :, None, :] == target[:, None, None, None],
        rank[None, :, None, :] == jnp.arange(CAP)[None, None, :, None],
    )
    mine_units = units_of(lengths[mine])
    mine_first = jnp.cumsum(mine_units, axis=1) - mine_units
    chosen = jnp.sum(jnp.where(hit, order, 0), axis=3).reshape(32, 2 * CAP)
    chosen_first = jnp.sum(jnp.where(hit, mine_first[None, :, None, :], 0), axis=3).reshape(32, 2 * CAP)
    from_half = (jnp.arange(2 * CAP, dtype=jnp.int32) // CAP)[None, :]
    unit = jnp.minimum(chosen_first[:, :, None] + jnp.arange(UNITS, dtype=jnp.int32), capacity - 1)
    block = ((unit // per_half) * SHARDS + shard) * 2 + from_half[:, :, None]
    cached_at = (block * per_half + unit % per_half).reshape(-1)
    fresh_at = (from_half * SHARDS)[:, :, None] + jnp.arange(SHARDS, dtype=jnp.int32)
    fresh_at = ((fresh_at * kv_heads + shard) * sessions + chosen[:, :, None]).reshape(-1)

    def deliver(rows, at):
        sent = jnp.take(rows, at, axis=0, mode="clip").reshape((32, -1) + rows.shape[1:])
        return lax.all_to_all(sent, COLUMN, split_axis=0, concat_axis=0, tiled=True)

    fresh_in = deliver(fresh_all.reshape(-1, 2, tokens, head), fresh_at).reshape(-1, SHARDS, 2, tokens, head)

    def deliver_cached(part):
        rows = part.shape[4]
        return deliver(part.reshape(-1, rows, head), cached_at).reshape(-1, UNITS, rows, head)

    all_sessions = jnp.arange(64 * sessions, dtype=jnp.int32)
    owned = new_owner[:, 0] == me
    place = jnp.cumsum(owned.astype(jnp.int32)) - 1
    is_slot = jnp.logical_and(owned[None, :], place[None, :] == order[:, None])

    def of_slot(per_session):
        return jnp.sum(jnp.where(is_slot, per_session[None, :], 0), axis=1)

    slot_session = of_slot(all_sessions)
    slot_hist, slot_new = of_slot(history_len), of_slot(new_len)
    holder = slot_session // sessions
    before = jnp.concatenate([jnp.full((1,), -1, jnp.int32), holder[:-1]])
    slot_rank = (holder == before).astype(jnp.int32)
    replicas = jnp.arange(64, dtype=jnp.int32)
    ingest_at = spread_index(replicas)
    holder_hit = ingest_source[None, :] == holder[:, None]
    ingester = jnp.sum(jnp.where(holder_hit, ingest_at[None, :], 0), axis=1)
    slot_from = (ingester % 32) * (2 * CAP) + (ingester // 32) * CAP + slot_rank

    own_source = ingest_source[me]
    own_hist = lax.dynamic_slice(history_len, (own_source * sessions,), (sessions,))
    own_new = lax.dynamic_slice(new_len, (own_source * sessions,), (sessions,))
    own_first = jnp.cumsum(units_of(own_hist)) - units_of(own_hist)
    meta = jnp.stack([half, shard]).astype(jnp.int32)
    slots = (slot_from, slot_hist, slot_new)
    early, fresh_in = tie((early, fresh_in))
    early_in = deliver_cached(early)
    weights = weigh(new_queries, early, fresh_all, norm_gains, own_hist, own_first, meta)
    migrated = build(0, [early_in], fresh_in, *slots)
    late, weights = tie((late, weights))
    late_in = deliver_cached(late)
    attended = mix(weights, early, late, fresh_all, own_new, own_first, meta, new_queries.shape[2])
    migrated = build(1, [early_in, late_in], fresh_in, *slots, into=migrated)
    return attended, migrated


def on_device(*arrays):
    history_len = arrays[6]
    sessions = arrays[0].shape[0]
    whole = sessions * UNITS
    short = whole * 11 // 14
    most = jnp.max(jnp.sum(units_of(history_len).reshape(64, sessions), axis=1))
    return lax.cond(most <= short, functools.partial(run, short), functools.partial(run, whole), *arrays)


def solution(mesh):
    split = Mesh(mesh.devices.reshape(4, 2, 4, 2, 4), ("x", "zh", "y", "core", "zl"))
    in_specs = (
        P(REPLICA, None, None, "zl"),
        P(REPLICA, "zl", None),
        P(REPLICA, "zl", None, None, None),
        P(),
        P(),
        P(),
        P(),
        P(),
    )
    out_specs = (P(REPLICA, "zl", None), P(REPLICA, None, None, "zl"))
    return jax.shard_map(on_device, mesh=split, in_specs=in_specs, out_specs=out_specs, check_vma=False)
```

time: 357 us -> 326 us (0.913)
  waiting for transfers between devices: 213 us -> 117 us
  blocking collectives: 0 us -> 84.5 us
  starting transfers between devices: 49.9 us -> 26.2 us
    all_to_all x0 -> x2, blocking collectives: none -> 84.5 us  [the longest x1 61.7 us: spread(): lax.all_to_all(part.reshape(64, -1, head), SPREAD, split_axis=0, concat_a...]
    all_to_all x2 -> x1, waiting for transfers between devices: 77.9 us -> 19 us  [spread(): lax.all_to_all(part.reshape(64, -1, head), SPREAD, split_axis=0, concat_a...]
    all_to_all x2 -> x1, waiting for transfers between devices: 29.6 us -> 4.05 us  [gather(): held = lax.all_to_all(picked, COLUMN, split_axis=0, concat_axis=1)]
    all_gather x3, waiting for transfers between devices: 77.4 us -> 60.2 us  [the longest x1 52.2 us: run(): lax.all_gather(early_held, RING, axis=0)]
    all_to_all x2 -> x1, starting transfers between devices: 20.3 us -> 5.66 us  [spread(): lax.all_to_all(part.reshape(64, -1, head), SPREAD, split_axis=0, concat_a...]
    all_to_all x2 -> x1, starting transfers between devices: 10.6 us -> 3.92 us  [gather(): held = lax.all_to_all(picked, COLUMN, split_axis=0, concat_axis=1)]
    all_to_all x3, waiting for transfers between devices: 28.2 us -> 34.2 us  [deliver(): return lax.all_to_all(sent, COLUMN, split_axis=0, concat_axis=0, tiled=True)]
    unnamed x27 -> x0, local copies, waits for them, and re-layouts: 5.59 us -> none
  transfers between devices with their start and end apart: 10 -> 8, of which waited for: 9 -> 6; matrix products, arithmetic and copies ran while one was open for 9% -> 10% of each run, Pallas kernels for 8% -> 10%
where the time goes in v3:
time: 326 us; the launch traced here: 325 us
  waiting for transfers between devices  117 us (36%)
  blocking collectives  84.5 us (26%)
  Pallas kernels  37.5 us (12%)
  local copies, waits for them, and re-layouts  36.8 us (11%)
  starting transfers between devices  26.2 us (8%)
  between operations  14.4 us (4%)
  other arithmetic  6.86 us (2%)
    all_to_all x1, blocking collectives, spread(): lax.all_to_all(part.reshape(64, -1, head), SPREAD, split_axis=0, concat_a...  61.7 us
    all_gather x1, waiting for transfers between devices, run(): lax.all_gather(early_held, RING, axis=0)  52.2 us
    all_to_all x3, waiting for transfers between devices, deliver(): return lax.all_to_all(sent, COLUMN, split_axis=0, concat_axis=0, tiled=True)  34.2 us
    all_to_all x1, blocking collectives, gather(): held = lax.all_to_all(picked, COLUMN, split_axis=0, concat_axis=1)  22.9 us
    all_to_all x1, waiting for transfers between devices, spread(): lax.all_to_all(part.reshape(64, -1, head), SPREAD, split_axis=0, concat_a...  19 us
    pallas_call x1, Pallas kernels, weigh(): pl.pallas_call(weigh_kernel, out_shape=jax.ShapeDtypeStruct((sessions, ro...  17.2 us
    all_to_all x3, starting transfers between devices, deliver(): return lax.all_to_all(sent, COLUMN, split_axis=0, concat_axis=0, tiled=True)  16.5 us
    gather x3, local copies, waits for them, and re-layouts, deliver(): jnp.take(rows, at, axis=0, mode='clip').reshape((32, -1) + rows.shape[1:])  15.7 us
  transfers between devices with their start and end apart: 8, of which 6 were waited for; matrix products, arithmetic and copies ran while one was open for 10% of the time, Pallas kernels for 10%

profile of v3, /device:TPU:1, one launch (start us, length us, event | category | flops | bytes accessed | tf_op | source)
XLA Modules:
  0.0 325.1 jit_solution(875389795221419836)
XLA Ops:
  7.2 0.7 add_select_fusion
  8.0 0.1 reduce_sum.189
  8.1 0.6 reduce_max.9
  9.4 309.1 %conditional.1 = (bf16[56,8,4096]{2,1,0:T(8,128)(2,1)}, bf16[56,2,96,128]{3,2,1,0:T(8,128)(2,1)}) conditional(s32[]{:T(128)} %convert_element_type.107, (s32[64]{0:T(128)}, s32[3584]{0:T(1024)}, s32[3584]{0:T(1024)}, bf16[56,2,64,128]{3,2,1,0:T(8,128)(2,1)}, bf16[56,8,4,2,128]{4,3,2,1,0:T(2,128)(2,1)}, /*index=5*/bf16[2,128]{1,0:T(2,128)(2,1)}, ...), branch_computations={%region_2.18_spmd, %region_18.34_spmd} | conditional | flops 7093781 | bytes 224652048 | solution.py:359
  9.7 1.2 dynamic_slice.20
  11.6 1.3 copy.175
  13.0 0.3 fusion.60
  13.8 0.1 reduce.9
  14.0 0.3 fusion.59
  14.3 1.1 maximum_bitcast_fusion.1
  15.5 0.8 gather_fusion.11
  16.3 0.8 gather_fusion.12
  17.0 0.8 fusion.117
  17.8 0.2 pad_maximum_fusion.1
  18.0 0.3 reshape.2034
  18.4 61.7 %all_to_all.88 = bf16[64,66,128]{2,1,0:T(8,128)(2,1)S(1)} all-to-all(bf16[64,66,128]{2,1,0:T(8,128)(2,1)S(1)} %reshape.2034), channel_id=1, replica_groups=mesh['x'=4,'zh'=2,'y'=4,'core'=2,'zl'=4] {'zh','x','y','core'}, dimensions={0} | all-to-all | bytes 2162688 | tf_op jit(solution)/shard_map/cond/branch_1_fun/all_to_all | solution.py:267
  80.1 0.8 reshape.2035
  80.9 5.7 %all-to-all-start.8 = ((bf16[64,22,128]{2,1,0:T(8,128)(2,1)}), bf16[64,22,128]{2,1,0:T(8,128)(2,1)S(1)}, u32[]{:S(2)}, u32[]{:S(2)}) async-start(bf16[64,22,128]{2,1,0:T(8,128)(2,1)} %reshape.2035), calls=%async_computation.8 | async-start | bytes 786432 | tf_op jit(solution)/shard_map/cond/branch_1_fun/all_to_all | solution.py:267
  86.7 0.8 gather_fusion.13
  87.8 0.8 gather_fusion.14
  88.6 0.8 copy.167
  89.4 19.0 %all-to-all-done.8 = bf16[64,22,128]{2,1,0:T(8,128)(2,1)S(1)} async-done(((bf16[64,22,128]{2,1,0:T(8,128)(2,1)}), bf16[64,22,128]{2,1,0:T(8,128)(2,1)S(1)}, u32[]{:S(2)}, u32[]{:S(2)}) %all-to-all-start.8) | async-done | bytes 360480 | tf_op jit(solution)/shard_map/cond/branch_1_fun/all_to_all | solution.py:267
  108.4 22.9 %all_to_all.89 = bf16[32,2,1,66,128]{4,1,3,2,0:T(2,128)(2,1)S(1)} all-to-all(bf16[32,2,1,66,128]{4,1,3,2,0:T(2,128)(2,1)S(1)} %copy.167), channel_id=1, replica_groups=mesh['x'=4,'zh'=2,'y'=4,'core'=2,'zl'=4] {'x','y','core'}, dimensions={0} | all-to-all | bytes 2162688 | tf_op jit(solution)/shard_map/cond/branch_1_fun/all_to_all | solution.py:271
  131.3 1.1 copy.171
  132.6 0.6 gather_fusion.16
  133.2 0.6 gather_fusion.19
  133.8 0.2 reduce_window_sum.58
  134.2 0.6 gather_fusion.17
  134.8 0.2 convert_reduce_fusion.2
  135.2 0.7 gather_fusion.15
  135.8 1.0 copy.169
  136.8 3.9 %all-to-all-start.10 = ((bf16[32,2,1,22,128]{4,1,3,2,0:T(2,128)(2,1)}), bf16[32,2,1,22,128]{4,1,3,2,0:T(2,128)(2,1)S(1)}, u32[]{:S(2)}, u32[]{:S(2)}) async-start(bf16[32,2,1,22,128]{4,1,3,2,0:T(2,128)(2,1)} %copy.169), calls=%async_computation.10 | async-start | bytes 720896 | tf_op jit(solution)/shard_map/cond/branch_1_fun/all_to_all | solution.py:271
  140.8 0.2 fusion.63
  141.2 0.1 reshape.2206
  141.3 5.4 %gather_fusion.18 = bf16[512,2,8,128]{3,2,1,0:T(8,128)(2,1)} fusion(bf16[1792,2,8,128]{3,2,1,0:T(8,128)(2,1)} %bitcast.143, s32[1024]{0:T(1024)S(1)} %pad_clamp_fusion.9), kind=kCustom, calls=%fused_computation.18 | custom fusion | bytes 4196352 | tf_op jit(solution)/shard_map/cond/branch_1_fun/jit(_take)/gather | solution.py:308
  146.8 4.0 %all-to-all-done.10 = bf16[32,2,1,22,128]{4,1,3,2,0:T(2,128)(2,1)S(1)} async-done(((bf16[32,2,1,22,128]{4,1,3,2,0:T(2,128)(2,1)}), bf16[32,2,1,22,128]{4,1,3,2,0:T(2,128)(2,1)S(1)}, u32[]{:S(2)}, u32[]{:S(2)}) %all-to-all-start.10) | async-done | bytes 360480 | tf_op jit(solution)/shard_map/cond/branch_1_fun/all_to_all | solution.py:271
  150.8 3.8 %all-to-all-start.11 = ((bf16[32,16,2,8,128]{4,3,2,1,0:T(8,128)(2,1)}), bf16[32,16,2,8,128]{4,3,2,1,0:T(8,128)(2,1)S(1)}, u32[]{:S(2)}, u32[]{:S(2)}) async-start(bf16[32,16,2,8,128]{4,3,2,1,0:T(8,128)(2,1)} %bitcast.148), calls=%async_computation.11 | async-start | bytes 4194304 | tf_op jit(solution)/shard_map/cond/branch_1_fun/all_to_all | solution.py:309
  154.7 0.8 copy.170
  155.6 0.1 fusion.64
  155.8 0.1 rem.891
  156.0 0.1 add.1248
  156.1 0.1 div.394
  156.2 0.1 sign_compare_fusion.1
  156.3 0.1 ne.1151
  156.5 26.3 %all-to-all-done.11 = bf16[32,16,2,8,128]{4,3,2,1,0:T(8,128)(2,1)S(1)} async-done(((bf16[32,16,2,8,128]{4,3,2,1,0:T(8,128)(2,1)}), bf16[32,16,2,8,128]{4,3,2,1,0:T(8,128)(2,1)S(1)}, u32[]{:S(2)}, u32[]{:S(2)}) %all-to-all-start.11) | async-done | bytes 2097184 | tf_op jit(solution)/shard_map/cond/branch_1_fun/all_to_all | solution.py:309
  182.8 52.2 %all-gather.19.cloned.1.call-done = bf16[16,88,24,128]{3,2,1,0:T(8,128)(2,1)} async-done(((bf16[2,88,24,128]{3,2,1,0:T(8,128)(2,1)}), bf16[16,88,24,128]{3,2,1,0:T(8,128)(2,1)}) %all-gather.19.cloned.1.call-update) | async-done | bytes 8650768 | tf_op jit(solution)/shard_map/cond/branch_1_fun/all_gather | solution.py:282
  235.0 6.4 %gather_fusion.20 = bf16[512,24,128]{2,1,0:T(8,128)(2,1)} fusion(bf16[1408,24,128]{2,1,0:T(8,128)(2,1)} %bitcast.137, s32[1024]{0:T(1024)S(1)} %pad_clamp_fusion.8), kind=kCustom, calls=%fused_computation.20 | custom fusion | bytes 6293504 | tf_op jit(solution)/shard_map/cond/branch_1_fun/jit(_take)/gather | solution.py:308
  241.5 7.7 %all-to-all-start.12 = ((bf16[32,16,24,128]{3,2,1,0:T(8,128)(2,1)}), bf16[32,16,24,128]{3,2,1,0:T(8,128)(2,1)S(1)}, u32[]{:S(2)}, u32[]{:S(2)}) async-start(bf16[32,16,24,128]{3,2,1,0:T(8,128)(2,1)} %bitcast.147), calls=%async_computation.12 | async-start | bytes 6291456 | tf_op jit(solution)/shard_map/cond/branch_1_fun/all_to_all | solution.py:309
  249.4 0.1 reduce.8
  249.5 0.3 reduce-window.54
  250.0 0.1 slice_reduce_fusion.1
  250.2 17.2 %branch_1_fun.4.w_ref = bf16[56,256,128]{2,1,0:T(8,128)(2,1)S(1)} custom-call(s32[2]{0:T(128)S(1)} %pad_add_fusion.1.meta, s32[56]{0:T(128)S(1)} %get-tuple-element.205.hist_len, s32[56]{0:T(128)S(1)} %sub.230.unit_first, bf16[56,8,4096]{2,1,0:T(8,128)(2,1)} %get-tuple-element.60.q_ref, bf16[2,4,2,88,24,128]{5,4,3,2,1,0:T(8,128)(2,1)} %bitcast.138, ...), custom_call_target="tpu_custom_call" | custom-call | tf_op jit(solution)/shard_map/cond/branch_1_fun/pallas_call | solution.py:135
  267.4 1.8 copy-done.10
  269.3 7.9 %all-gather.17.cloned.1.call-done = bf16[8,2,88,8,128]{4,3,2,1,0:T(8,128)(2,1)} async-done(((bf16[1,2,88,8,128]{4,3,2,1,0:T(8,128)(2,1)}), bf16[8,2,88,8,128]{4,3,2,1,0:T(8,128)(2,1)}) %all-gather.17.cloned.1.call-update) | async-done | bytes 2883600 | tf_op jit(solution)/shard_map/cond/branch_1_fun/all_gather | solution.py:283
  277.2 3.9 %gather_fusion.21 = bf16[512,8,128]{2,1,0:T(8,128)(2,1)} fusion(bf16[1408,8,128]{2,1,0:T(8,128)(2,1)} %bitcast.132, s32[1024]{0:T(1024)S(1)} %pad_clamp_fusion.8), kind=kCustom, calls=%fused_computation.21 | custom fusion | bytes 2099200 | tf_op jit(solution)/shard_map/cond/branch_1_fun/jit(_take)/gather | solution.py:308
  281.0 7.8 %all-to-all-done.12 = bf16[32,16,24,128]{3,2,1,0:T(8,128)(2,1)S(1)} async-done(((bf16[32,16,24,128]{3,2,1,0:T(8,128)(2,1)}), bf16[32,16,24,128]{3,2,1,0:T(8,128)(2,1)S(1)}, u32[]{:S(2)}, u32[]{:S(2)}) %all-to-all-start.12) | async-done | bytes 3145760 | tf_op jit(solution)/shard_map/cond/branch_1_fun/all_to_all | solution.py:309
  288.9 5.0 %all-to-all-start.13 = ((bf16[32,16,8,128]{3,2,1,0:T(8,128)(2,1)}), bf16[32,16,8,128]{3,2,1,0:T(8,128)(2,1)}, u32[]{:S(2)}, u32[]{:S(2)}) async-start(bf16[32,16,8,128]{3,2,1,0:T(8,128)(2,1)} %bitcast.161), calls=%async_computation.13 | async-start | bytes 2097152 | tf_op jit(solution)/shard_map/cond/branch_1_fun/all_to_all | solution.py:309
  294.0 0.6 select_reduce_fusion.5
  294.6 0.2 select_reduce_fusion.9
  294.9 1.8 copy-done.11
  296.7 10.7 %branch_1_fun.5 = bf16[56,8,4096]{2,1,0:T(8,128)(2,1)} custom-call(s32[2]{0:T(128)S(1)} %pad_add_fusion.1.meta, s32[56]{0:T(128)S(1)} %dynamic_slice.21.new_len, s32[56]{0:T(128)S(1)} %sub.230.unit_first, bf16[56,256,128]{2,1,0:T(8,128)(2,1)} %copy-done.10, bf16[2,4,2,88,24,128]{5,4,3,2,1,0:T(8,128)(2,1)} %bitcast.139, ...), custom_call_target="tpu_custom_call" | custom-call | tf_op jit(solution)/shard_map/cond/branch_1_fun/pallas_call | solution.py:158
  307.4 3.9 %branch_1_fun.6.refs_3_ = bf16[56,2,96,128]{3,2,1,0:T(8,128)(2,1)} custom-call(s32[56]{0:T(128)S(1)} %fusion.100.slot_from, s32[56]{0:T(128)S(1)} %get-tuple-element.194.hist_len, s32[56]{0:T(128)S(1)} %get-tuple-element.193.new_len, bf16[128,4,24,128]{3,2,1,0:T(8,128)(2,1)S(1)} %bitcast.126, bf16[128,4,2,8,128]{4,3,2,1,0:T(8,128)(2,1)S(1)} %bitcast.128), custom_call_target="tpu_custom_call" | custom-call | tf_op jit(solution)/shard_map/cond/branch_1_fun/pallas_call | solution.py:220
  311.4 1.6 copy-done.4
  312.9 5.6 %branch_1_fun.7 = bf16[56,2,96,128]{3,2,1,0:T(8,128)(2,1)} custom-call(s32[56]{0:T(128)S(1)} %fusion.100.slot_from, s32[56]{0:T(128)S(1)} %get-tuple-element.194.hist_len, s32[56]{0:T(128)S(1)} %get-tuple-element.193.new_len, bf16[128,4,24,128]{3,2,1,0:T(8,128)(2,1)} %bitcast.127, ...), custom_call_target="tpu_custom_call", output_to_operand_aliasing={{}: (6, {})} | custom-call | tf_op jit(solution)/shard_map/cond/branch_1_fun/pallas_call | solution.py:220
  (87 shorter events, 2.9 us)
Async XLA Ops:
  9.6 3.7 %copy-start.25 = (bf16[2,128]{1,0:T(2,128)(2,1)S(1)}, bf16[2,128]{1,0:T(2,128)(2,1)}, u32[]{:S(2)}) copy-start(bf16[2,128]{1,0:T(2,128)(2,1)} %get-tuple-element.55.gain_ref) | copy-start | bytes 1540 | tf_op jit(solution)/shard_map/cond
  9.6 3.9 %copy-start.19 = (s32[3584]{0:T(1024)S(1)}, s32[3584]{0:T(1024)}, u32[]{:S(2)}) copy-start(s32[3584]{0:T(1024)} %get-tuple-element.52) | copy-start | bytes 43012 | tf_op jit(solution)/shard_map/cond
  9.7 131.7 %all-gather.21.cloned.1.call-start = ((), (), s32[]{:S(2)}) async-start(), calls=%async_computation.19 | async-start | bytes 8257536 | tf_op jit(solution)/shard_map/cond/branch_1_fun/all_gather | solution.py:258
  13.3 2.2 copy-start.15
  18.0 62.0 %copy-start.17 = (bf16[176,8,128]{2,1,0:T(8,128)(2,1)S(1)}, bf16[176,8,128]{2,1,0:T(8,128)(2,1)}, u32[]{:S(2)}) copy-start(bf16[176,8,128]{2,1,0:T(8,128)(2,1)} %get-tuple-element.57) | copy-start | bytes 1081348 | tf_op jit(solution)/shard_map/cond
  18.4 68.3 %copy-start.13 = (s32[64]{0:T(128)S(1)}, s32[64]{0:T(128)}, u32[]{:S(2)}) copy-start(s32[64]{0:T(128)} %get-tuple-element.51) | copy-start | bytes 772 | tf_op jit(solution)/shard_map/cond
  80.9 27.5 %all-to-all-start.8 = ((bf16[64,22,128]{2,1,0:T(8,128)(2,1)}), bf16[64,22,128]{2,1,0:T(8,128)(2,1)S(1)}, u32[]{:S(2)}, u32[]{:S(2)}) async-start(bf16[64,22,128]{2,1,0:T(8,128)(2,1)} %reshape.2035), calls=%async_computation.8 | async-start | bytes 786432 | tf_op jit(solution)/shard_map/cond/branch_1_fun/all_to_all | solution.py:267
  86.6 148.5 %all-gather.19.cloned.1.call-start = ((), (), s32[]{:S(2)}) async-start(), calls=%async_computation.18 | async-start | bytes 9732096 | tf_op jit(solution)/shard_map/cond/branch_1_fun/all_gather | solution.py:282
  131.3 2.8 copy-start.21
  136.8 14.0 %all-to-all-start.10 = ((bf16[32,2,1,22,128]{4,1,3,2,0:T(2,128)(2,1)}), bf16[32,2,1,22,128]{4,1,3,2,0:T(2,128)(2,1)S(1)}, u32[]{:S(2)}, u32[]{:S(2)}) async-start(bf16[32,2,1,22,128]{4,1,3,2,0:T(2,128)(2,1)} %copy.169), calls=%async_computation.10 | async-start | bytes 720896 | tf_op jit(solution)/shard_map/cond/branch_1_fun/all_to_all | solution.py:271
  150.8 32.0 %all-to-all-start.11 = ((bf16[32,16,2,8,128]{4,3,2,1,0:T(8,128)(2,1)}), bf16[32,16,2,8,128]{4,3,2,1,0:T(8,128)(2,1)S(1)}, u32[]{:S(2)}, u32[]{:S(2)}) async-start(bf16[32,16,2,8,128]{4,3,2,1,0:T(8,128)(2,1)} %bitcast.148), calls=%async_computation.11 | async-start | bytes 4194304 | tf_op jit(solution)/shard_map/cond/branch_1_fun/all_to_all | solution.py:309
  154.7 122.5 %all-gather.17.cloned.1.call-start = ((), (), s32[]{:S(2)}) async-start(), calls=%async_computation.17 | async-start | bytes 3244032 | tf_op jit(solution)/shard_map/cond/branch_1_fun/all_gather | solution.py:283
  182.8 58.6 %copy-start.2 = (bf16[32,16,2,8,128]{4,3,2,1,0:T(8,128)(2,1)}, bf16[32,16,2,8,128]{4,3,2,1,0:T(8,128)(2,1)S(1)}, u32[]{:S(2)}) copy-start(bf16[32,16,2,8,128]{4,3,2,1,0:T(8,128)(2,1)S(1)} %all-to-all-done.11) | copy-start | bytes 6291460 | tf_op jit(solution)/shard_map/cond
  241.5 7.7 %copy-start.23 = (s32[3584]{0:T(1024)S(1)}, s32[3584]{0:T(1024)}, u32[]{:S(2)}) copy-start(s32[3584]{0:T(1024)} %get-tuple-element.50) | copy-start | bytes 43012 | tf_op jit(solution)/shard_map/cond
  241.5 47.4 %all-to-all-start.12 = ((bf16[32,16,24,128]{3,2,1,0:T(8,128)(2,1)}), bf16[32,16,24,128]{3,2,1,0:T(8,128)(2,1)S(1)}, u32[]{:S(2)}, u32[]{:S(2)}) async-start(bf16[32,16,24,128]{3,2,1,0:T(8,128)(2,1)} %bitcast.147), calls=%async_computation.12 | async-start | bytes 6291456 | tf_op jit(solution)/shard_map/cond/branch_1_fun/all_to_all | solution.py:309
  267.4 1.8 copy-start.10
  288.9 18.5 %copy-start.1 = (bf16[32,16,24,128]{3,2,1,0:T(8,128)(2,1)}, bf16[32,16,24,128]{3,2,1,0:T(8,128)(2,1)S(1)}, u32[]{:S(2)}) copy-start(bf16[32,16,24,128]{3,2,1,0:T(8,128)(2,1)S(1)} %all-to-all-done.12) | copy-start | bytes 9437188 | tf_op jit(solution)/shard_map/cond
  288.9 22.5 %all-to-all-start.13 = ((bf16[32,16,8,128]{3,2,1,0:T(8,128)(2,1)}), bf16[32,16,8,128]{3,2,1,0:T(8,128)(2,1)}, u32[]{:S(2)}, u32[]{:S(2)}) async-start(bf16[32,16,8,128]{3,2,1,0:T(8,128)(2,1)} %bitcast.161), calls=%async_computation.13 | async-start | bytes 2097152 | tf_op jit(solution)/shard_map/cond/branch_1_fun/all_to_all | solution.py:309
  294.9 1.8 copy-start.11
  296.7 10.7 %copy-start.3 = (bf16[32,16,2,8,128]{4,3,2,1,0:T(8,128)(2,1)S(1)}, bf16[32,16,2,8,128]{4,3,2,1,0:T(8,128)(2,1)}, u32[]{:S(2)}) copy-start(bf16[32,16,2,8,128]{4,3,2,1,0:T(8,128)(2,1)} %copy-done.2) | copy-start | bytes 6291460 | tf_op jit(solution)/shard_map/cond
  311.4 1.6 copy-start.4
Sparse Core Ops, SparseCore 0:
  15.6 121.8 all-gather.20
  139.8 95.1 all-gather.18
  236.8 40.2 all-gather.16
